TPU v7x, 32 devices: a whole 2x2x4 slice. The times are simulated.
32 devices in a mesh: ctx: 8 (over z, y), head: 4 (over x, core).
Axes of the slice: x: 2, y: 2, z: 4, core: 2. Of those that a mesh axis runs over, the one named last changes fastest.
Arguments:
- tokens: bfloat16 [1024, 2048], P('ctx'), may hold values from -6 to 6
- grad_out: bfloat16 [1024, 2048], P('ctx'), may hold values from -6 to 6
- expert_ids: int32 [1024, 8], P('ctx'), may hold values from 0 to 15, all different within a row; in each aligned block of 128 rows (0 to 127, 128 to 255, ...) at most 80 rows name the same one
- gate_probs: bfloat16 [1024, 8], P('ctx'), may hold values from 0.029907227 to 0.3984375
- w_gate: bfloat16 [16, 768, 2048], P('ctx', 'head'), may hold values from -0.125 to 0.125
- w_up: bfloat16 [16, 768, 2048], P('ctx', 'head'), may hold values from -0.125 to 0.125
- w_down: bfloat16 [16, 768, 2048], P('ctx', 'head'), may hold values from -0.21875 to 0.21875
- query_rows: bfloat16 [1024, 4096], P('ctx', 'head'), may hold values from -4.5 to 4.5, as said below
- key_rows: bfloat16 [1024, 512], P('ctx', 'head'), may hold values from -4.5 to 4.5, as said below
- value_rows: bfloat16 [1024, 512], P('ctx', 'head'), may hold values from -6 to 6
- attn_out: bfloat16 [1024, 4096], P('ctx', 'head'), may hold values from -6 to 6
- grad_attn: bfloat16 [1024, 4096], P('ctx', 'head'), may hold values from -6 to 6
- segment_ids: int32 [1024], replicated, may hold values from 0 to 7, never falling along the last dimension, each value on 1 to 384 neighbouring positions
Outputs:
- grad_tokens: bfloat16 [1024, 2048], P('ctx')
- grad_gate: bfloat16 [16, 768, 2048], P('ctx', 'head')
- grad_up: bfloat16 [16, 768, 2048], P('ctx', 'head')
- grad_down: bfloat16 [16, 768, 2048], P('ctx', 'head')
- grad_query: bfloat16 [1024, 4096], P('ctx', 'head')
- grad_key: bfloat16 [1024, 512], P('ctx', 'head')
- grad_value: bfloat16 [1024, 512], P('ctx', 'head')
Inputs may be any that keep to these rules, and one draw needn't show every extreme that they name: `expert_ids`: each row names different experts; among the 128 tokens of one index of ctx no expert is named more than 80 times, a bound that some block reaches. `segment_ids`: ids never fall; a document has at most 384 positions, and one has exactly that many. `query_rows`: entries stay within the range. `key_rows`: entries stay within the range.
All inputs are finite; a program needn't handle non-finite values.
Results may differ from a plain program's by a relative error of at most 0.0057.
Values may be sent and summed in bfloat16 or wider, within the bound.
A program may use at most 128 MiB of HBM per device.

v0:
```python
import jax
import jax.numpy as jnp
from jax import lax
from jax.sharding import PartitionSpec as P

HQ = 32
KVH = 4
HD = 128
REACH = 3


def passed_along(block, axis, distance):
    devices = range(lax.axis_size(axis))
    route = [(i - distance, i) for i in devices if i - distance in devices]
    return lax.ppermute(block, axis, route)


def expert_backward(recv_rows, recv_grads, w_gate, w_up, w_down):
    gate_pre = jnp.einsum("secd,efd->secf", recv_rows, w_gate, preferred_element_type=jnp.float32)
    up_pre = jnp.einsum("secd,efd->secf", recv_rows, w_up, preferred_element_type=jnp.float32)
    sigmoid_gate = jax.nn.sigmoid(gate_pre)
    active = gate_pre * sigmoid_gate
    hidden = (active * up_pre).astype(jnp.bfloat16)
    hidden_grad = jnp.einsum(
        "secd,efd->secf", recv_grads, w_down, preferred_element_type=jnp.float32
    )
    gate_grad = (
        hidden_grad * up_pre * sigmoid_gate * (1.0 + gate_pre * (1.0 - sigmoid_gate))
    ).astype(jnp.bfloat16)
    up_grad = (hidden_grad * active).astype(jnp.bfloat16)
    back_rows = jnp.einsum(
        "secf,efd->secd", gate_grad, w_gate, preferred_element_type=jnp.float32
    ) + jnp.einsum("secf,efd->secd", up_grad, w_up, preferred_element_type=jnp.float32)
    grad_gate = jnp.einsum(
        "secf,secd->efd", gate_grad, recv_rows, preferred_element_type=jnp.float32
    ).astype(jnp.bfloat16)
    grad_up = jnp.einsum(
        "secf,secd->efd", up_grad, recv_rows, preferred_element_type=jnp.float32
    ).astype(jnp.bfloat16)
    grad_down = jnp.einsum(
        "secf,secd->efd", hidden, recv_grads, preferred_element_type=jnp.float32
    ).astype(jnp.bfloat16)
    return (back_rows, grad_gate, grad_up, grad_down)


def pair_total(returned, slot_index, tok_count, top_count):
    flat_rows = returned.reshape(-1, returned.shape[3])
    picked = flat_rows[slot_index]
    return jnp.sum(picked.reshape(tok_count, top_count, returned.shape[3]), axis=1)


def body(
    tokens,
    grad_out,
    expert_ids,
    gate_probs,
    w_gate,
    w_up,
    w_down,
    query_rows,
    key_rows,
    value_rows,
    attn_out,
    grad_attn,
    segment_ids,
):
    tok_count, width = tokens.shape
    top_count = expert_ids.shape[1]
    ctx_count = lax.axis_size("ctx")
    local_experts = w_gate.shape[0]
    total_experts = local_experts * ctx_count
    capacity = (5 * tok_count * top_count + 4 * total_experts - 1) // (4 * total_experts)
    pair_count = tok_count * top_count
    flat_expert = expert_ids.reshape(pair_count)
    onehot = (flat_expert[:, None] == jnp.arange(total_experts, dtype=jnp.int32)[None, :]).astype(
        jnp.int32
    )
    earlier = jnp.cumsum(onehot, axis=0) - onehot
    slot_rank = jnp.sum(earlier * onehot, axis=1)
    slot_index = flat_expert * capacity + slot_rank
    slot_pair = (
        jnp.full((total_experts * capacity,), pair_count, jnp.int32)
        .at[slot_index]
        .set(jnp.arange(pair_count, dtype=jnp.int32))
    )
    slot_token = slot_pair // top_count
    padded_tokens = jnp.concatenate([tokens, jnp.zeros((1, width), tokens.dtype)], axis=0)
    padded_grad = jnp.concatenate([grad_out, jnp.zeros((1, width), grad_out.dtype)], axis=0)
    padded_probs = jnp.concatenate(
        [gate_probs.reshape(pair_count).astype(jnp.float32), jnp.zeros((1,), jnp.float32)]
    )
    buffer_shape = (ctx_count, local_experts, capacity, width)
    send_rows = padded_tokens[slot_token].reshape(buffer_shape)
    send_grads = (
        (padded_probs[slot_pair][:, None] * padded_grad[slot_token].astype(jnp.float32))
        .astype(jnp.bfloat16)
        .reshape(buffer_shape)
    )
    recv_rows, recv_grads = (
        lax.all_to_all(send_rows, "ctx", split_axis=0, concat_axis=0, tiled=True),
        lax.all_to_all(send_grads, "ctx", split_axis=0, concat_axis=0, tiled=True),
    )
    back_rows, grad_gate, grad_up, grad_down = expert_backward(
        recv_rows, recv_grads, w_gate, w_up, w_down
    )
    shared = lax.psum_scatter(back_rows, "head", scatter_dimension=3, tiled=True)
    returned = lax.all_to_all(shared, "ctx", split_axis=0, concat_axis=0, tiled=True)
    summed = pair_total(returned, slot_index, tok_count, top_count)
    grad_tokens = lax.all_gather(summed.astype(jnp.bfloat16), "head", axis=1, tiled=True)
    att_rows = query_rows.shape[0]
    kv_width = key_rows.shape[1]
    kv_local = kv_width // HD
    group_size = HQ // KVH
    window = (REACH + 1) * att_rows
    score_scale = HD ** (-0.5)
    ctx_index = lax.axis_index("ctx")
    key_blocks = []
    value_blocks = []
    for distance in range(REACH, 0, -1):
        far_key, far_value = passed_along((key_rows, value_rows), "ctx", distance)
        key_blocks.append(far_key)
        value_blocks.append(far_value)
    window_key = jnp.concatenate(key_blocks + [key_rows], axis=0).reshape(window, kv_local, HD)
    window_value = jnp.concatenate(value_blocks + [value_rows], axis=0).reshape(
        window, kv_local, HD
    )
    query_pos = ctx_index * att_rows + jnp.arange(att_rows, dtype=jnp.int32)
    key_pos = (ctx_index - REACH) * att_rows + jnp.arange(window, dtype=jnp.int32)
    padded_segment = jnp.concatenate([jnp.full((REACH * att_rows,), -1, jnp.int32), segment_ids])
    key_seg = lax.dynamic_slice_in_dim(padded_segment, ctx_index * att_rows, window, 0)
    query_seg = lax.dynamic_slice_in_dim(segment_ids, ctx_index * att_rows, att_rows, 0)
    visible = (key_pos[None, :] <= query_pos[:, None]) & (key_seg[None, :] == query_seg[:, None])
    query_heads = query_rows.reshape(att_rows, kv_local, group_size, HD)
    out_heads = attn_out.reshape(att_rows, kv_local, group_size, HD)
    grad_heads = grad_attn.reshape(att_rows, kv_local, group_size, HD)
    scores = (
        jnp.einsum("ajgd,tjd->jgat", query_heads, window_key, preferred_element_type=jnp.float32)
        * score_scale
    )
    row_peak = jnp.max(jnp.where(visible, scores, -jnp.inf), axis=-1, keepdims=True)
    weights_exp = jnp.exp(jnp.where(visible, scores - row_peak, -jnp.inf))
    probs = weights_exp / jnp.sum(weights_exp, axis=-1, keepdims=True)
    row_delta = jnp.einsum(
        "ajgd,ajgd->jga", grad_heads, out_heads, preferred_element_type=jnp.float32
    )
    prob_grad = jnp.einsum(
        "ajgd,tjd->jgat", grad_heads, window_value, preferred_element_type=jnp.float32
    )
    score_grad = (probs * (prob_grad - row_delta[..., None])).astype(jnp.bfloat16)
    probs_low = probs.astype(jnp.bfloat16)
    grad_query = (
        (
            score_scale
            * jnp.einsum(
                "jgat,tjd->ajgd", score_grad, window_key, preferred_element_type=jnp.float32
            )
        )
        .astype(jnp.bfloat16)
        .reshape(att_rows, -1)
    )
    key_terms = (
        score_scale
        * jnp.einsum("jgat,ajgd->tjd", score_grad, query_heads, preferred_element_type=jnp.float32)
    ).reshape(window, kv_width)
    value_terms = jnp.einsum(
        "jgat,ajgd->tjd", probs_low, grad_heads, preferred_element_type=jnp.float32
    ).reshape(window, kv_width)
    key_total = key_terms[REACH * att_rows :]
    value_total = value_terms[REACH * att_rows :]
    for distance in range(1, REACH + 1):
        offset = (REACH - distance) * att_rows
        got_key, got_value = passed_along(
            (key_terms[offset : offset + att_rows], value_terms[offset : offset + att_rows]),
            "ctx",
            -distance,
        )
        key_total = key_total + got_key
        value_total = value_total + got_value
    return (
        grad_tokens,
        grad_gate,
        grad_up,
        grad_down,
        grad_query,
        key_total.astype(jnp.bfloat16),
        value_total.astype(jnp.bfloat16),
    )


def solution(mesh):
    placed = (
        P("ctx", None),
        P("ctx", None),
        P("ctx", None),
        P("ctx", None),
        P("ctx", "head", None),
        P("ctx", "head", None),
        P("ctx", "head", None),
        P("ctx", "head"),
        P("ctx", "head"),
        P("ctx", "head"),
        P("ctx", "head"),
        P("ctx", "head"),
        P(),
    )
    return jax.shard_map(
        body,
        mesh=mesh,
        in_specs=placed,
        out_specs=(
            P("ctx", None),
            P("ctx", "head", None),
            P("ctx", "head", None),
            P("ctx", "head", None),
            P("ctx", "head"),
            P("ctx", "head"),
            P("ctx", "head"),
        ),
        check_vma=False,
    )
```

profile of v0, /device:TPU:25, one launch (start us, length us, event | category | flops | bytes accessed | tf_op | source)
XLA Modules:
  0.0 489.9 jit_solution(5273955249189059517)
XLA Ops:
  7.2 0.8 broadcast_multiply_fusion
  8.0 0.8 copy.48
  9.2 4.5 reduce-window.6
  14.2 4.3 scatter_custom_fusion
  18.5 1.1 concatenate.24
  19.6 6.1 %gather_fusion.2 = bf16[1280,2048]{1,0:T(8,128)(2,1)} fusion(bf16[129,2048]{1,0:T(8,128)(2,1)S(1)} %concatenate.24, s32[2048]{0:T(1024)S(1)} %get-tuple-element.40), kind=kCustom, calls=%fused_computation.2 | custom fusion | bytes 10490880 | tf_op jit(solution)/shard_map/gather | solution.py:93
  25.7 5.6 %all-to-all-start.1 = ((bf16[8,2,80,2048]{3,2,1,0:T(8,128)(2,1)}), bf16[8,2,80,2048]{3,2,1,0:T(8,128)(2,1)}, u32[]{:S(2)}, u32[]{:S(2)}) async-start(bf16[8,2,80,2048]{3,2,1,0:T(8,128)(2,1)} %bitcast.213), calls=%async_computation.1 | async-start | bytes 10485760 | tf_op jit(solution)/shard_map/all_to_all | solution.py:100
  31.6 7.1 %gather_fusion = f32[1280]{0:T(1024)S(1)} fusion(f32[1025]{0:T(1024)S(1)} %maximum_convert_fusion, s32[2048]{0:T(1024)S(1)} %get-tuple-element.41), kind=kCustom, calls=%fused_computation | custom fusion | bytes 15360 | tf_op jit(solution)/shard_map/gather | solution.py:95
  38.8 6.1 %gather_fusion.1 = bf16[1280,2048]{1,0:T(8,128)(2,1)} fusion(bf16[129,2048]{1,0:T(8,128)(2,1)S(1)} %concatenate.23, s32[2048]{0:T(1024)S(1)} %get-tuple-element.40), kind=kCustom, calls=%fused_computation.1 | custom fusion | bytes 10490880 | tf_op jit(solution)/shard_map/gather | solution.py:95
  45.0 5.8 %fusion = bf16[8,2,80,2048]{3,2,1,0:T(8,128)(2,1)} fusion(bf16[8,2,80,2048]{3,2,1,0:T(8,128)(2,1)} %bitcast.214, f32[8,2,80]{2,1,0:T(2,128)S(1)} %mul.101), kind=kLoop, calls=%fused_computation.6 | loop fusion | flops 7864320 | bytes 10490880 | tf_op jit(solution)/shard_map/convert_element_type | solution.py:96
  50.7 95.6 %all-to-all-done.1 = bf16[8,2,80,2048]{3,2,1,0:T(8,128)(2,1)} async-done(((bf16[8,2,80,2048]{3,2,1,0:T(8,128)(2,1)}), bf16[8,2,80,2048]{3,2,1,0:T(8,128)(2,1)}, u32[]{:S(2)}, u32[]{:S(2)}) %all-to-all-start.1) | async-done | bytes 5242912 | tf_op jit(solution)/shard_map/all_to_all | solution.py:100
  146.3 4.6 all-to-all-start
  151.2 5.2 %fusion.37 = f32[8,2,80,192]{3,2,0,1:T(8,128)} fusion(bf16[2,192,2048]{2,1,0:T(8,128)(2,1)S(1)} %copy-done, bf16[8,2,80,2048]{3,2,1,0:T(8,128)(2,1)} %all-to-all-done.1), kind=kOutput, calls=%fused_computation.41 | convolution fusion | flops 1006632960 | bytes 7798784 | tf_op jit(solution)/shard_map/secd,efd->secf/dot_general | solution.py:19
  156.4 5.1 %fusion.32 = f32[8,2,80,192]{3,2,0,1:T(8,128)} fusion(bf16[2,192,2048]{2,1,0:T(8,128)(2,1)S(1)} %copy-done.2, bf16[8,2,80,2048]{3,2,1,0:T(8,128)(2,1)} %all-to-all-done.1), kind=kOutput, calls=%fused_computation.40 | convolution fusion | flops 1006632960 | bytes 7798784 | tf_op jit(solution)/shard_map/secd,efd->secf/dot_general | solution.py:20
  161.5 104.4 %all-to-all-done = bf16[8,2,80,2048]{3,2,1,0:T(8,128)(2,1)} async-done(((bf16[8,2,80,2048]{3,2,1,0:T(8,128)(2,1)}), bf16[8,2,80,2048]{3,2,1,0:T(8,128)(2,1)}, u32[]{:S(2)}, u32[]{:S(2)}) %all-to-all-start) | async-done | bytes 5242912 | tf_op jit(solution)/shard_map/all_to_all | solution.py:101
  265.9 5.6 %multiply_convert_fusion.1 = (bf16[8,2,80,192]{3,2,0,1:T(8,128)(2,1)S(1)}, bf16[8,2,80,192]{3,2,0,1:T(8,128)(2,1)S(1)}) fusion(f32[8,2,80,192]{3,2,0,1:T(8,128)} %fusion.37, f32[8,2,80,192]{3,2,0,1:T(8,128)} %fusion.32, bf16[2,192,2048]{2,1,0:T(8,128)(2,1)} %param.19, bf16[8,2,80,2048]{3,2,1,0:T(8,128)(2,1)} %all-to-all-done), kind=kOutput, calls=%fused_computation.45 | convolution fusion | flops 1009827840 | bytes 9764864 | tf_op jit(solution)/shard_map/secd,efd->secf/dot_general | solution.py:24
  271.5 1.5 fusion.26
  273.0 5.6 %add_bitcast_fusion = f32[8,2,80,2048]{3,2,0,1:T(8,128)} fusion(f32[2,8,80,2048]{3,2,1,0:T(8,128)S(1)} %fusion.26, bf16[8,2,80,192]{3,2,0,1:T(8,128)(2,1)S(1)} %get-tuple-element.28, bf16[2,192,2048]{2,1,0:T(8,128)(2,1)S(1)} %copy-done.2), kind=kOutput, calls=%fused_computation.7 | convolution fusion | flops 1009254400 | bytes 23035904 | tf_op jit(solution)/shard_map/secf,efd->secd/dot_general | solution.py:33
  278.6 0.7 copy-done.14
  279.4 1.3 collective-permute-start.4
  280.6 1.3 collective-permute-start.3
  282.0 1.3 collective-permute-start.1
  283.3 1.3 collective-permute-start
  284.6 2.3 collective-permute-start.2
  287.6 76.4 %reduce-scatter.2.cloned.1.call-done = f32[8,2,80,512]{3,2,0,1:T(8,128)} async-done(((f32[8,2,80,2048]{3,2,0,1:T(8,128)}), f32[8,2,80,512]{3,2,0,1:T(8,128)}) %reduce-scatter.2.cloned.1.call-update) | async-done | bytes 2621456 | tf_op jit(solution)/shard_map/reduce_scatter | solution.py:106
  364.1 3.6 copy.55
  367.6 5.6 %all-to-all-start.2 = ((f32[8,2,80,512]{3,2,1,0:T(8,128)}), f32[8,2,80,512]{3,2,1,0:T(8,128)}, u32[]{:S(2)}, u32[]{:S(2)}) async-start(f32[8,2,80,512]{3,2,1,0:T(8,128)} %copy.55), calls=%async_computation.3 | async-start | bytes 5242880 | tf_op jit(solution)/shard_map/all_to_all | solution.py:107
  373.2 3.1 collective-permute-start.5
  377.3 33.1 %collective-permute-done.5 = bf16[128,128]{1,0:T(8,128)(2,1)S(1)} collective-permute-done((bf16[128,128]{1,0:T(8,128)(2,1)S(1)}, bf16[128,128]{1,0:T(8,128)(2,1)S(1)}, u32[]{:S(2)}, u32[]{:S(2)}) %collective-permute-start.5) | collective-permute-done | bytes 32800 | tf_op jit(solution)/shard_map/ppermute | solution.py:15
  410.4 0.8 fusion.47
  411.6 1.9 collective-permute-start.6
  413.5 23.5 %collective-permute-start.8 = (f32[128,128]{1,0:T(8,128)S(1)}, f32[128,128]{1,0:T(8,128)S(1)}, u32[]{:S(2)}, u32[]{:S(2)}) collective-permute-start(f32[128,128]{1,0:T(8,128)S(1)} %get-tuple-element.34), channel_id=1, source_target_pairs={{12,0},{16,4},{20,8},{24,12},{28,16},{13,1},{17,5},{21,9},{25,13},... | collective-permute-start | bytes 196616 | tf_op jit(solution)/shard_map/ppermute | solution.py:15
  437.0 3.2 collective-permute-start.7
  440.5 0.6 convolution_bitcast_fusion
  441.2 0.8 copy.65
  442.1 2.5 collective-permute-start.9
  444.5 1.3 collective-permute-start.11
  445.8 2.0 collective-permute-start.10
  447.9 0.6 fusion.82
  448.5 0.7 collective-permute-done.10
  449.2 0.6 fusion.78
  449.8 5.1 %bitcast_convert_fusion.1 = bf16[2,192,2048]{2,1,0:T(8,128)(2,1)} fusion(bf16[8,2,80,192]{3,2,0,1:T(8,128)(2,1)S(1)} %copy-done.6, bf16[8,2,80,2048]{3,2,1,0:T(8,128)(2,1)} %all-to-all-done.1), kind=kOutput, calls=%fused_computation.21 | convolution fusion | flops 1007419392 | bytes 7307264 | tf_op jit(solution)/shard_map/secf,secd->efd/dot_general | solution.py:37
  454.9 5.2 %bitcast_convert_fusion.2 = bf16[2,192,2048]{2,1,0:T(8,128)(2,1)} fusion(bf16[8,2,80,192]{3,2,0,1:T(8,128)(2,1)S(1)} %copy-done.4, bf16[8,2,80,2048]{3,2,1,0:T(8,128)(2,1)} %all-to-all-done.1), kind=kOutput, calls=%fused_computation.22 | convolution fusion | flops 1007419392 | bytes 7307264 | tf_op jit(solution)/shard_map/secf,secd->efd/dot_general | solution.py:34
  460.1 5.2 %bitcast_convert_fusion = bf16[2,192,2048]{2,1,0:T(8,128)(2,1)} fusion(bf16[8,2,80,2048]{3,2,1,0:T(8,128)(2,1)} %all-to-all-done, f32[8,2,80,192]{3,2,0,1:T(8,128)S(1)} %copy-done.16, f32[8,2,80,192]{3,2,0,1:T(8,128)S(1)} %copy-done.15), kind=kOutput, calls=%fused_computation.20 | convolution fusion | flops 1008893952 | bytes 8781824 | tf_op jit(solution)/shard_map/secf,secd->efd/dot_general | solution.py:40
  465.3 7.2 %gather_fusion.3 = f32[1024,512]{1,0:T(8,128)} fusion(f32[1280,512]{1,0:T(8,128)} %bitcast.19, s32[1024]{0:T(1024)S(1)} %broadcast_clamp_fusion), kind=kCustom, calls=%fused_computation.3 | custom fusion | bytes 4198400 | tf_op jit(solution)/shard_map/gather | solution.py:48
  472.5 2.1 bitcast_reduce_fusion
  474.6 7.7 %all_gather.3 = bf16[128,2048]{1,0:T(8,128)(2,1)S(1)} all-gather(bf16[128,512]{1,0:T(8,128)(2,1)S(1)} %bitcast_reduce_fusion), channel_id=1, replica_groups=mesh['ctx'=8,'head'=4] {'head'}, dimensions={1}, use_global_device_ids=true | all-gather | bytes 655360 | tf_op jit(solution)/shard_map/all_gather | solution.py:109
  482.3 0.8 copy.134
  (82 shorter events, 4.0 us)
Async XLA Ops:
  7.2 144.0 %copy-start = (bf16[2,192,2048]{2,1,0:T(8,128)(2,1)S(1)}, bf16[2,192,2048]{2,1,0:T(8,128)(2,1)}, u32[]{:S(2)}) copy-start(bf16[2,192,2048]{2,1,0:T(8,128)(2,1)} %param.17) | copy-start | bytes 4718596
  25.7 5.6 %copy-start.13 = (bf16[128,8]{0,1:T(8,128)(2,1)S(1)}, bf16[128,8]{0,1:T(8,128)(2,1)}, u32[]{:S(2)}) copy-start(bf16[128,8]{0,1:T(8,128)(2,1)} %param.16) | copy-start | bytes 6148
  25.7 120.6 %all-to-all-start.1 = ((bf16[8,2,80,2048]{3,2,1,0:T(8,128)(2,1)}), bf16[8,2,80,2048]{3,2,1,0:T(8,128)(2,1)}, u32[]{:S(2)}, u32[]{:S(2)}) async-start(bf16[8,2,80,2048]{3,2,1,0:T(8,128)(2,1)} %bitcast.213), calls=%async_computation.1 | async-start | bytes 10485760 | tf_op jit(solution)/shard_map/all_to_all | solution.py:100
  31.6 7.2 %copy-start.7 = (bf16[128,2048]{1,0:T(8,128)(2,1)S(1)}, bf16[128,2048]{1,0:T(8,128)(2,1)}, u32[]{:S(2)}) copy-start(bf16[128,2048]{1,0:T(8,128)(2,1)} %param.14) | copy-start | bytes 1572868
  146.3 119.6 %all-to-all-start = ((bf16[8,2,80,2048]{3,2,1,0:T(8,128)(2,1)}), bf16[8,2,80,2048]{3,2,1,0:T(8,128)(2,1)}, u32[]{:S(2)}, u32[]{:S(2)}) async-start(bf16[8,2,80,2048]{3,2,1,0:T(8,128)(2,1)} %fusion), calls=%async_computation | async-start | bytes 10485760 | tf_op jit(solution)/shard_map/all_to_all | solution.py:101
  150.9 5.5 %copy-start.2 = (bf16[2,192,2048]{2,1,0:T(8,128)(2,1)S(1)}, bf16[2,192,2048]{2,1,0:T(8,128)(2,1)}, u32[]{:S(2)}) copy-start(bf16[2,192,2048]{2,1,0:T(8,128)(2,1)} %param.18) | copy-start | bytes 4718596
  150.9 213.1 %reduce-scatter.2.cloned.1.call-start = ((), (), s32[]{:S(2)}) async-start(), calls=%async_computation.4 | async-start | bytes 13107200 | tf_op jit(solution)/shard_map/reduce_scatter | solution.py:106
  271.4 1.6 copy-start.3
  271.5 1.6 copy-start.5
  278.6 0.8 copy-start.14
  278.6 3.3 copy-start.11
  278.6 8.3 %copy-start.8 = (bf16[128,1024]{1,0:T(8,128)(2,1)S(1)}, bf16[128,1024]{1,0:T(8,128)(2,1)}, u32[]{:S(2)}) copy-start(bf16[128,1024]{1,0:T(8,128)(2,1)} %param.23) | copy-start | bytes 786436
  278.6 8.3 %copy-start.9 = (bf16[128,1024]{1,0:T(8,128)(2,1)S(1)}, bf16[128,1024]{1,0:T(8,128)(2,1)}, u32[]{:S(2)}) copy-start(bf16[128,1024]{1,0:T(8,128)(2,1)} %param.24) | copy-start | bytes 786436
  278.6 8.4 %copy-start.12 = (s32[1024]{0:T(1024)S(1)}, s32[1024]{0:T(1024)}, u32[]{:S(2)}) copy-start(s32[1024]{0:T(1024)} %param.25) | copy-start | bytes 12292
  279.4 97.9 %collective-permute-start.4 = (bf16[128,128]{1,0:T(8,128)(2,1)S(1)}, bf16[128,128]{1,0:T(8,128)(2,1)S(1)}, u32[]{:S(2)}, u32[]{:S(2)}) collective-permute-start(bf16[128,128]{1,0:T(8,128)(2,1)S(1)} %copy-done.14), channel_id=1, source_target_pairs={{0,8},{4,12},{8,16},{12,20},{16,24},{20,28},{1,9},{5,13},{9,17},{1... | collective-permute-start | bytes 98312 | tf_op jit(solution)/shard_map/ppermute | solution.py:15
  280.6 96.6 %collective-permute-start.3 = (bf16[128,128]{1,0:T(8,128)(2,1)S(1)}, bf16[128,128]{1,0:T(8,128)(2,1)S(1)}, u32[]{:S(2)}, u32[]{:S(2)}) collective-permute-start(bf16[128,128]{1,0:T(8,128)(2,1)S(1)} %copy-done.14), channel_id=1, source_target_pairs={{0,12},{4,16},{8,20},{12,24},{16,28},{1,13},{5,17},{9,21},{13,25},... | collective-permute-start | bytes 98312 | tf_op jit(solution)/shard_map/ppermute | solution.py:15
  282.0 91.3 %collective-permute-start.1 = (bf16[128,128]{1,0:T(8,128)(2,1)S(1)}, bf16[128,128]{1,0:T(8,128)(2,1)S(1)}, u32[]{:S(2)}, u32[]{:S(2)}) collective-permute-start(bf16[128,128]{1,0:T(8,128)(2,1)S(1)} %copy-done.11), channel_id=1, source_target_pairs={{0,8},{4,12},{8,16},{12,20},{16,24},{20,28},{1,9},{5,13},{9,17},{1... | collective-permute-start | bytes 98312 | tf_op jit(solution)/shard_map/ppermute | solution.py:15
  283.3 93.1 %collective-permute-start = (bf16[128,128]{1,0:T(8,128)(2,1)S(1)}, bf16[128,128]{1,0:T(8,128)(2,1)S(1)}, u32[]{:S(2)}, u32[]{:S(2)}) collective-permute-start(bf16[128,128]{1,0:T(8,128)(2,1)S(1)} %copy-done.11), channel_id=1, source_target_pairs={{0,12},{4,16},{8,20},{12,24},{16,28},{1,13},{5,17},{9,21},{13,25},... | collective-permute-start | bytes 98312 | tf_op jit(solution)/shard_map/ppermute | solution.py:15
  284.6 91.8 %collective-permute-start.2 = (bf16[128,128]{1,0:T(8,128)(2,1)S(1)}, bf16[128,128]{1,0:T(8,128)(2,1)S(1)}, u32[]{:S(2)}, u32[]{:S(2)}) collective-permute-start(bf16[128,128]{1,0:T(8,128)(2,1)S(1)} %copy-done.11), channel_id=1, source_target_pairs={{0,4},{4,8},{8,12},{12,16},{16,20},{20,24},{24,28},{1,5},{5,9},{9,... | collective-permute-start | bytes 98312 | tf_op jit(solution)/shard_map/ppermute | solution.py:15
  367.6 8.7 %copy-start.10 = (bf16[128,1024]{1,0:T(8,128)(2,1)S(1)}, bf16[128,1024]{1,0:T(8,128)(2,1)}, u32[]{:S(2)}) copy-start(bf16[128,1024]{1,0:T(8,128)(2,1)} %param.20) | copy-start | bytes 786436
  367.6 97.7 %all-to-all-start.2 = ((f32[8,2,80,512]{3,2,1,0:T(8,128)}), f32[8,2,80,512]{3,2,1,0:T(8,128)}, u32[]{:S(2)}, u32[]{:S(2)}) async-start(f32[8,2,80,512]{3,2,1,0:T(8,128)} %copy.55), calls=%async_computation.3 | async-start | bytes 5242880 | tf_op jit(solution)/shard_map/all_to_all | solution.py:107
  373.2 37.2 %collective-permute-start.5 = (bf16[128,128]{1,0:T(8,128)(2,1)S(1)}, bf16[128,128]{1,0:T(8,128)(2,1)S(1)}, u32[]{:S(2)}, u32[]{:S(2)}) collective-permute-start(bf16[128,128]{1,0:T(8,128)(2,1)S(1)} %copy-done.14), channel_id=1, source_target_pairs={{0,4},{4,8},{8,12},{12,16},{16,20},{20,24},{24,28},{1,5},{5,9},{9,... | collective-permute-start | bytes 98312 | tf_op jit(solution)/shard_map/ppermute | solution.py:15
  411.6 34.2 %collective-permute-start.6 = (f32[128,128]{1,0:T(8,128)S(1)}, f32[128,128]{1,0:T(8,128)S(1)}, u32[]{:S(2)}, u32[]{:S(2)}) collective-permute-start(f32[128,128]{1,0:T(8,128)S(1)} %get-tuple-element.33), channel_id=1, source_target_pairs={{4,0},{8,4},{12,8},{16,12},{20,16},{24,20},{28,24},{5,1},{9,5},{13... | collective-permute-start | bytes 196616 | tf_op jit(solution)/shard_map/ppermute | solution.py:15
  413.5 34.3 %collective-permute-start.8 = (f32[128,128]{1,0:T(8,128)S(1)}, f32[128,128]{1,0:T(8,128)S(1)}, u32[]{:S(2)}, u32[]{:S(2)}) collective-permute-start(f32[128,128]{1,0:T(8,128)S(1)} %get-tuple-element.34), channel_id=1, source_target_pairs={{12,0},{16,4},{20,8},{24,12},{28,16},{13,1},{17,5},{21,9},{25,13},... | collective-permute-start | bytes 196616 | tf_op jit(solution)/shard_map/ppermute | solution.py:15
  437.0 10.8 %collective-permute-start.7 = (f32[128,128]{1,0:T(8,128)S(1)}, f32[128,128]{1,0:T(8,128)S(1)}, u32[]{:S(2)}, u32[]{:S(2)}) collective-permute-start(f32[128,128]{1,0:T(8,128)S(1)} %get-tuple-element.35), channel_id=1, source_target_pairs={{8,0},{12,4},{16,8},{20,12},{24,16},{28,20},{9,1},{13,5},{17,9},{2... | collective-permute-start | bytes 196616 | tf_op jit(solution)/shard_map/ppermute | solution.py:15
  440.5 9.3 %copy-start.6 = (bf16[8,2,80,192]{3,2,0,1:T(8,128)(2,1)S(1)}, bf16[8,2,80,192]{3,2,0,1:T(8,128)(2,1)}, u32[]{:S(2)}) copy-start(bf16[8,2,80,192]{3,2,0,1:T(8,128)(2,1)} %copy-done.5) | copy-start | bytes 1474564
  442.1 6.4 %collective-permute-start.9 = (f32[128,128]{1,0:T(8,128)S(1)}, f32[128,128]{1,0:T(8,128)S(1)}, u32[]{:S(2)}, u32[]{:S(2)}) collective-permute-start(f32[128,128]{1,0:T(8,128)S(1)} %get-tuple-element.30), channel_id=1, source_target_pairs={{4,0},{8,4},{12,8},{16,12},{20,16},{24,20},{28,24},{5,1},{9,5},{13... | collective-permute-start | bytes 196616 | tf_op jit(solution)/shard_map/ppermute | solution.py:15
  444.5 4.0 collective-permute-start.11
  445.8 3.3 collective-permute-start.10
  449.8 5.1 %copy-start.4 = (bf16[8,2,80,192]{3,2,0,1:T(8,128)(2,1)S(1)}, bf16[8,2,80,192]{3,2,0,1:T(8,128)(2,1)}, u32[]{:S(2)}) copy-start(bf16[8,2,80,192]{3,2,0,1:T(8,128)(2,1)} %copy-done.3) | copy-start | bytes 1474564
  454.9 5.2 %copy-start.15 = (f32[8,2,80,192]{3,2,0,1:T(8,128)S(1)}, f32[8,2,80,192]{3,2,0,1:T(8,128)}, u32[]{:S(2)}) copy-start(f32[8,2,80,192]{3,2,0,1:T(8,128)} %fusion.37) | copy-start | bytes 2949124
  454.9 5.2 %copy-start.16 = (f32[8,2,80,192]{3,2,0,1:T(8,128)S(1)}, f32[8,2,80,192]{3,2,0,1:T(8,128)}, u32[]{:S(2)}) copy-start(f32[8,2,80,192]{3,2,0,1:T(8,128)} %fusion.32) | copy-start | bytes 2949124
  465.3 17.8 %copy-start.1 = (bf16[2,192,2048]{2,1,0:T(8,128)(2,1)S(1)}, bf16[2,192,2048]{2,1,0:T(8,128)(2,1)}, u32[]{:S(2)}) copy-start(bf16[2,192,2048]{2,1,0:T(8,128)(2,1)} %param.17) | copy-start | bytes 4718596
Sparse Core Ops, SparseCore 0:
  278.8 85.2 reduce-scatter.1
where the time goes:
time: 494 us; the launch traced here: 490 us
  waiting for transfers between devices  310 us (63%)
  starting transfers between devices  60.9 us (12%)
  matrix products  41.1 us (8%)
  local copies, waits for them, and re-layouts  39.9 us (8%)
  other arithmetic  15.6 us (3%)
  between operations  14.5 us (3%)
  blocking collectives  7.7 us (2%)
    all_to_all x1, waiting for transfers between devices, body(): lax.all_to_all(send_grads, 'ctx', split_axis=0, concat_axis=0, tiled=True)  104 us
    all_to_all x1, waiting for transfers between devices, body(): lax.all_to_all(send_rows, 'ctx', split_axis=0, concat_axis=0, tiled=True)  95.6 us
    reduce_scatter x1, waiting for transfers between devices, body(): lax.psum_scatter(back_rows, 'head', scatter_dimension=3, tiled=True)  76.4 us
    ppermute x12, starting transfers between devices, passed_along(): return lax.ppermute(block, axis, route)  44.8 us
    ppermute x12, waiting for transfers between devices, passed_along(): return lax.ppermute(block, axis, route)  33.8 us
  transfers between devices with their start and end apart: 16, of which 5 were waited for; matrix products, arithmetic and copies ran while one was open for 11% of the time, Pallas kernels for 0%

commit v1 on v0

--- a/solution.py
+++ b/solution.py
@@ -47,6 +47,98 @@
     flat_rows = returned.reshape(-1, returned.shape[3])
     picked = flat_rows[slot_index]
     return jnp.sum(picked.reshape(tok_count, top_count, returned.shape[3]), axis=1)
+
+
+def routed_experts(tokens, grad_out, expert_ids, gate_probs, w_gate, w_up, w_down):
+    tok_count, width = tokens.shape
+    top_count = expert_ids.shape[1]
+    ctx_count = lax.axis_size("ctx")
+    local_experts = w_gate.shape[0]
+    total_experts = local_experts * ctx_count
+    capacity = (5 * tok_count * top_count + 4 * total_experts - 1) // (4 * total_experts)
+    pair_count = tok_count * top_count
+    flat_expert = expert_ids.reshape(pair_count)
+    onehot = (flat_expert[:, None] == jnp.arange(total_experts, dtype=jnp.int32)[None, :]).astype(
+        jnp.int32
+    )
+    earlier = jnp.cumsum(onehot, axis=0) - onehot
+    slot_rank = jnp.sum(earlier * onehot, axis=1)
+    slot_index = flat_expert * capacity + slot_rank
+    slot_pair = (
+        jnp.full((total_experts * capacity,), pair_count, jnp.int32)
+        .at[slot_index]
+        .set(jnp.arange(pair_count, dtype=jnp.int32))
+    )
+    slot_token = slot_pair // top_count
+    padded_tokens = jnp.concatenate([tokens, jnp.zeros((1, width), tokens.dtype)], axis=0)
+    padded_grad = jnp.concatenate([grad_out, jnp.zeros((1, width), grad_out.dtype)], axis=0)
+    padded_probs = jnp.concatenate(
+        [gate_probs.reshape(pair_count).astype(jnp.float32), jnp.zeros((1,), jnp.float32)]
+    )
+    buffer_shape = (ctx_count, local_experts, capacity, width)
+    send_rows = padded_tokens[slot_token].reshape(buffer_shape)
+    send_grads = (
+        (padded_probs[slot_pair][:, None] * padded_grad[slot_token].astype(jnp.float32))
+        .astype(jnp.bfloat16)
+        .reshape(buffer_shape)
+    )
+    recv_rows, recv_grads = (
+        lax.all_to_all(send_rows, "ctx", split_axis=0, concat_axis=0, tiled=True),
+        lax.all_to_all(send_grads, "ctx", split_axis=0, concat_axis=0, tiled=True),
+    )
+    back_rows, grad_gate, grad_up, grad_down = expert_backward(
+        recv_rows, recv_grads, w_gate, w_up, w_down
+    )
+    shared = lax.psum_scatter(back_rows, "head", scatter_dimension=3, tiled=True)
+    returned = lax.all_to_all(shared, "ctx", split_axis=0, concat_axis=0, tiled=True)
+    summed = pair_total(returned, slot_index, tok_count, top_count)
+    grad_tokens = lax.all_gather(summed.astype(jnp.bfloat16), "head", axis=1, tiled=True)
+    return grad_tokens, grad_gate, grad_up, grad_down
+
+
+def dense_experts(tokens, grad_out, expert_ids, gate_probs, w_gate, w_up, w_down):
+    ctx_count = lax.axis_size("ctx")
+    local_experts = w_gate.shape[0]
+    total_experts = local_experts * ctx_count
+    chosen = expert_ids[:, :, None] == jnp.arange(total_experts, dtype=jnp.int32)[None, None, :]
+    prob_table = jnp.sum(
+        jnp.where(chosen, gate_probs.astype(jnp.float32)[:, :, None], 0.0), axis=1
+    )
+    all_tokens = lax.all_gather(tokens, "ctx", axis=0, tiled=True)
+    all_grads = lax.all_gather(grad_out, "ctx", axis=0, tiled=True)
+    all_probs = lax.all_gather(prob_table, "ctx", axis=0, tiled=True)
+    my_probs = lax.dynamic_slice_in_dim(
+        all_probs, lax.axis_index("ctx") * local_experts, local_experts, 1
+    )
+    pair_grads = (my_probs.T[:, :, None] * all_grads.astype(jnp.float32)[None]).astype(jnp.bfloat16)
+    gate_pre = jnp.einsum("td,efd->etf", all_tokens, w_gate, preferred_element_type=jnp.float32)
+    up_pre = jnp.einsum("td,efd->etf", all_tokens, w_up, preferred_element_type=jnp.float32)
+    sigmoid_gate = jax.nn.sigmoid(gate_pre)
+    active = gate_pre * sigmoid_gate
+    hidden = (active * up_pre).astype(jnp.bfloat16)
+    hidden_grad = jnp.einsum("etd,efd->etf", pair_grads, w_down, preferred_element_type=jnp.float32)
+    gate_grad = (
+        hidden_grad * up_pre * sigmoid_gate * (1.0 + gate_pre * (1.0 - sigmoid_gate))
+    ).astype(jnp.bfloat16)
+    up_grad = (hidden_grad * active).astype(jnp.bfloat16)
+    back = jnp.einsum(
+        "etf,efd->td", gate_grad, w_gate, preferred_element_type=jnp.float32
+    ) + jnp.einsum("etf,efd->td", up_grad, w_up, preferred_element_type=jnp.float32)
+    shared = lax.psum_scatter(
+        back.astype(jnp.bfloat16), "head", scatter_dimension=1, tiled=True
+    )
+    summed = lax.psum_scatter(shared, "ctx", scatter_dimension=0, tiled=True)
+    grad_tokens = lax.all_gather(summed.astype(jnp.bfloat16), "head", axis=1, tiled=True)
+    grad_gate = jnp.einsum(
+        "etf,td->efd", gate_grad, all_tokens, preferred_element_type=jnp.float32
+    ).astype(jnp.bfloat16)
+    grad_up = jnp.einsum(
+        "etf,td->efd", up_grad, all_tokens, preferred_element_type=jnp.float32
+    ).astype(jnp.bfloat16)
+    grad_down = jnp.einsum(
+        "etf,etd->efd", hidden, pair_grads, preferred_element_type=jnp.float32
+    ).astype(jnp.bfloat16)
+    return grad_tokens, grad_gate, grad_up, grad_down
 
 
 def body(
@@ -69,44 +161,15 @@
     ctx_count = lax.axis_size("ctx")
     local_experts = w_gate.shape[0]
     total_experts = local_experts * ctx_count
-    capacity = (5 * tok_count * top_count + 4 * total_experts - 1) // (4 * total_experts)
-    pair_count = tok_count * top_count
-    flat_expert = expert_ids.reshape(pair_count)
-    onehot = (flat_expert[:, None] == jnp.arange(total_experts, dtype=jnp.int32)[None, :]).astype(
-        jnp.int32
-    )
-    earlier = jnp.cumsum(onehot, axis=0) - onehot
-    slot_rank = jnp.sum(earlier * onehot, axis=1)
-    slot_index = flat_expert * capacity + slot_rank
-    slot_pair = (
-        jnp.full((total_experts * capacity,), pair_count, jnp.int32)
-        .at[slot_index]
-        .set(jnp.arange(pair_count, dtype=jnp.int32))
-    )
-    slot_token = slot_pair // top_count
-    padded_tokens = jnp.concatenate([tokens, jnp.zeros((1, width), tokens.dtype)], axis=0)
-    padded_grad = jnp.concatenate([grad_out, jnp.zeros((1, width), grad_out.dtype)], axis=0)
-    padded_probs = jnp.concatenate(
-        [gate_probs.reshape(pair_count).astype(jnp.float32), jnp.zeros((1,), jnp.float32)]
-    )
-    buffer_shape = (ctx_count, local_experts, capacity, width)
-    send_rows = padded_tokens[slot_token].reshape(buffer_shape)
-    send_grads = (
-        (padded_probs[slot_pair][:, None] * padded_grad[slot_token].astype(jnp.float32))
-        .astype(jnp.bfloat16)
-        .reshape(buffer_shape)
-    )
-    recv_rows, recv_grads = (
-        lax.all_to_all(send_rows, "ctx", split_axis=0, concat_axis=0, tiled=True),
-        lax.all_to_all(send_grads, "ctx", split_axis=0, concat_axis=0, tiled=True),
-    )
-    back_rows, grad_gate, grad_up, grad_down = expert_backward(
-        recv_rows, recv_grads, w_gate, w_up, w_down
-    )
-    shared = lax.psum_scatter(back_rows, "head", scatter_dimension=3, tiled=True)
-    returned = lax.all_to_all(shared, "ctx", split_axis=0, concat_axis=0, tiled=True)
-    summed = pair_total(returned, slot_index, tok_count, top_count)
-    grad_tokens = lax.all_gather(summed.astype(jnp.bfloat16), "head", axis=1, tiled=True)
+    if tok_count > local_experts * ((5 * tok_count * top_count + 4 * total_experts - 1) // (4 * total_experts)):
+        expert_outputs = routed_experts(
+            tokens, grad_out, expert_ids, gate_probs, w_gate, w_up, w_down
+        )
+    else:
+        expert_outputs = dense_experts(
+            tokens, grad_out, expert_ids, gate_probs, w_gate, w_up, w_down
+        )
+    grad_tokens, grad_gate, grad_up, grad_down = expert_outputs
     att_rows = query_rows.shape[0]
     kv_width = key_rows.shape[1]
     kv_local = kv_width // HD

time: 494 us -> 300 us (0.61)
  waiting for transfers between devices: 310 us -> 177 us
  local copies, waits for them, and re-layouts: 39.9 us -> 4.72 us
  starting transfers between devices: 60.9 us -> 27.8 us
  blocking collectives: 7.7 us -> 31.9 us
  matrix products: 41.1 us -> 33.1 us
  other arithmetic: 15.6 us -> 7.86 us
    all_to_all x3 -> x0, waiting for transfers between devices: 200 us -> none  [the longest x1 104 us: body(): lax.all_to_all(send_grads, 'ctx', split_axis=0, concat_axis=0, tiled=True)]
    all_gather x0 -> x2, waiting for transfers between devices: none -> 116 us  [the longest x1 65.5 us: dense_experts(): all_grads = lax.all_gather(grad_out, 'ctx', axis=0, tiled=True)]
    ppermute x12, waiting for transfers between devices: 33.8 us -> 3.27 us  [passed_along(): return lax.ppermute(block, axis, route)]
    gather x4 -> x0, local copies, waits for them, and re-layouts: 26.4 us -> none  [the longest x1 7.16 us: pair_total(): picked = flat_rows[slot_index]]
    all_gather x1 -> x2, blocking collectives: 7.7 us -> 31.9 us  [the longest x1 22.4 us: dense_experts(): all_probs = lax.all_gather(prob_table, 'ctx', axis=0, tiled=True)]
    reduce_scatter x1 -> x2, waiting for transfers between devices: 76.4 us -> 56.2 us  [the longest x1 47.3 us: dense_experts(): summed = lax.psum_scatter(shared, 'ctx', scatter_dimension=0, tiled=True)]
    ppermute x12, starting transfers between devices: 44.8 us -> 27.7 us  [passed_along(): return lax.ppermute(block, axis, route)]
    all_to_all x3 -> x0, starting transfers between devices: 15.8 us -> none  [the longest x1 5.63 us: body(): lax.all_to_all(send_rows, 'ctx', split_axis=0, concat_axis=0, tiled=True)]
  transfers between devices with their start and end apart: 16 -> 16, of which waited for: 5 -> 7; matrix products, arithmetic and copies ran while one was open for 11% -> 10% of each run, Pallas kernels for 0% -> 0%
where the time goes in v1:
time: 300 us; the launch traced here: 297 us
  waiting for transfers between devices  177 us (59%)
  matrix products  33.1 us (11%)
  blocking collectives  31.9 us (11%)
  starting transfers between devices  27.8 us (9%)
  between operations  14.2 us (5%)
  other arithmetic  7.86 us (3%)
  local copies, waits for them, and re-layouts  4.72 us (2%)
    all_gather x1, waiting for transfers between devices, dense_experts(): all_grads = lax.all_gather(grad_out, 'ctx', axis=0, tiled=True)  65.5 us
    all_gather x1, waiting for transfers between devices, dense_experts(): all_tokens = lax.all_gather(tokens, 'ctx', axis=0, tiled=True)  50.8 us
    reduce_scatter x1, waiting for transfers between devices, dense_experts(): summed = lax.psum_scatter(shared, 'ctx', scatter_dimension=0, tiled=True)  47.3 us
    ppermute x12, starting transfers between devices, passed_along(): return lax.ppermute(block, axis, route)  27.7 us
    all_gather x1, blocking collectives, dense_experts(): all_probs = lax.all_gather(prob_table, 'ctx', axis=0, tiled=True)  22.4 us
    all_gather x1, blocking collectives, dense_experts(): lax.all_gather(summed.astype(jnp.bfloat16), 'head', axis=1, tiled=True)  9.56 us
    reduce_scatter x1, waiting for transfers between devices, dense_experts(): lax.psum_scatter(back.astype(jnp.bfloat16), 'head', scatter_dimension=1,...  8.95 us
  transfers between devices with their start and end apart: 16, of which 7 were waited for; matrix products, arithmetic and copies ran while one was open for 10% of the time, Pallas kernels for 0%

profile of v1, /device:TPU:25, one launch (start us, length us, event | category | flops | bytes accessed | tf_op | source)
XLA Modules:
  0.0 296.9 jit_solution(5679499148780976846)
XLA Ops:
  7.2 0.7 all-gather.5.cloned.1.call-update
  8.0 0.7 all-gather.3.cloned.1.call-update
  8.7 0.7 convert_element_type.51
  9.4 0.7 select_reduce_fusion
  10.1 22.4 %all_gather.12 = f32[1024,16]{0,1:T(8,128)S(1)} all-gather(f32[128,16]{0,1:T(8,128)S(1)} %select_reduce_fusion), channel_id=1, replica_groups=mesh['ctx'=8,'head'=4] {'ctx'}, dimensions={0}, use_global_device_ids=true | all-gather | bytes 73728 | tf_op jit(solution)/shard_map/all_gather | solution.py:109
  32.5 50.8 %all-gather.5.cloned.1.call-done = bf16[1024,2048]{1,0:T(8,128)(2,1)} async-done(((bf16[128,2048]{1,0:T(8,128)(2,1)}), bf16[1024,2048]{1,0:T(8,128)(2,1)}) %all-gather.5.cloned.1.call-update) | async-done | bytes 4194320 | tf_op jit(solution)/shard_map/all_gather | solution.py:107
  83.3 5.3 %fusion.11 = f32[2,192,1024]{2,1,0:T(8,128)} fusion(bf16[2,192,2048]{2,1,0:T(8,128)(2,1)S(1)} %copy-done, bf16[1024,2048]{1,0:T(8,128)(2,1)} %all-gather.5.cloned.1.call-done), kind=kOutput, calls=%fused_computation.13 | convolution fusion | flops 1610612736 | bytes 7340032 | tf_op jit(solution)/shard_map/td,efd->etf/dot_general | solution.py:114
  88.6 3.0 %fusion.13 = f32[2,192,1024]{2,1,0:T(8,128)} fusion(bf16[2,192,2048]{2,1,0:T(8,128)(2,1)S(1)} %copy-done.18, bf16[1024,2048]{1,0:T(8,128)(2,1)S(1)} %copy-done.16), kind=kOutput, calls=%fused_computation.15 | convolution fusion | flops 1610612736 | bytes 7340032 | tf_op jit(solution)/shard_map/td,efd->etf/dot_general | solution.py:115
  91.6 65.5 %all-gather.3.cloned.1.call-done = bf16[1024,2048]{1,0:T(8,128)(2,1)} async-done(((bf16[128,2048]{1,0:T(8,128)(2,1)}), bf16[1024,2048]{1,0:T(8,128)(2,1)}) %all-gather.3.cloned.1.call-update) | async-done | bytes 4194320 | tf_op jit(solution)/shard_map/all_gather | solution.py:108
  157.2 3.4 %convert_element_type.52 = f32[1024,2048]{1,0:T(8,128)S(1)} convert(bf16[1024,2048]{1,0:T(8,128)(2,1)} %all-gather.3.cloned.1.call-done) | non-fusion elementwise | flops 2097152 | bytes 12582912 | tf_op jit(solution)/shard_map/convert_element_type | solution.py:113
  160.6 3.6 %multiply_convert_fusion.5 = (bf16[2,1024,192]{1,2,0:T(8,128)(2,1)S(1)}, bf16[2,1024,192]{1,2,0:T(8,128)(2,1)S(1)}) fusion(f32[2,192,1024]{2,1,0:T(8,128)S(1)} %copy-done.3, f32[2,192,1024]{2,1,0:T(8,128)S(1)} %copy-done.5, bf16[2,192,2048]{2,1,0:T(8,128)(2,1)S(1)} %copy-done.2, f32[1024,2048]{1,0:T(8,128)S(1)} %convert_element_type.52, ...), kind=kOutput, calls=%fused_computation.43 | convolution fusion | flops 1624113152 | bytes 14688256 | tf_op jit(solution)/shard_map/etd,efd->etf/dot_general | solution.py:119
  164.3 2.4 fusion.75
  166.7 4.3 %fusion.2 = bf16[1024,2048]{1,0:T(8,128)(2,1)} fusion(f32[1024,2048,1]{1,0,2:T(8,128)S(1)} %fusion.75, bf16[2,1024,192]{1,2,0:T(8,128)(2,1)S(1)} %get-tuple-element.21, bf16[2,192,2048]{2,1,0:T(8,128)(2,1)S(1)} %copy-done.19), kind=kOutput, calls=%fused_computation.4 | convolution fusion | flops 1614807040 | bytes 14942208 | tf_op jit(solution)/shard_map/etf,efd->td/dot_general | solution.py:126
  171.2 0.6 copy-done.20
  171.8 1.3 collective-permute-start.4
  173.1 1.3 collective-permute-start.3
  174.4 1.3 collective-permute-start.1
  175.7 1.3 collective-permute-start
  177.0 2.1 collective-permute-start.2
  179.9 0.7 collective-permute-done.1
  180.6 2.1 collective-permute-start.5
  182.7 0.7 collective-permute-done
  183.4 0.4 fusion.24
  183.9 0.4 fusion.28
  184.4 1.8 collective-permute-done.5
  186.2 0.8 fusion.37
  187.0 0.4 fusion.40
  187.4 0.7 slice_bitcast_fusion.6
  188.1 3.8 %collective-permute-start.6 = (f32[128,128]{1,0:T(8,128)}, f32[128,128]{1,0:T(8,128)S(1)}, u32[]{:S(2)}, u32[]{:S(2)}) collective-permute-start(f32[128,128]{1,0:T(8,128)} %get-tuple-element.26), channel_id=1, source_target_pairs={{4,0},{8,4},{12,8},{16,12},{20,16},{24,20},{28,24},{5,1},{9,5},{13... | collective-permute-start | bytes 196616 | tf_op jit(solution)/shard_map/ppermute | solution.py:15
  191.9 6.3 %collective-permute-start.8 = (f32[128,128]{1,0:T(8,128)}, f32[128,128]{1,0:T(8,128)}, u32[]{:S(2)}, u32[]{:S(2)}) collective-permute-start(f32[128,128]{1,0:T(8,128)} %get-tuple-element.27), channel_id=1, source_target_pairs={{12,0},{16,4},{20,8},{24,12},{28,16},{13,1},{17,5},{21,9},{25,13},... | collective-permute-start | bytes 196616 | tf_op jit(solution)/shard_map/ppermute | solution.py:15
  198.2 1.9 collective-permute-start.7
  200.1 0.3 fusion.38
  200.4 0.6 convolution_bitcast_fusion
  201.1 0.6 slice_bitcast_fusion.2
  201.7 0.8 copy.35
  202.6 2.8 collective-permute-start.9
  205.4 1.3 collective-permute-start.11
  206.7 8.9 %reduce-scatter.3.cloned.1.call-done = bf16[1024,512]{1,0:T(8,128)(2,1)} async-done(((bf16[1024,2048]{1,0:T(8,128)(2,1)}), bf16[1024,512]{1,0:T(8,128)(2,1)}) %reduce-scatter.3.cloned.1.call-update) | async-done | bytes 1048592 | tf_op jit(solution)/shard_map/reduce_scatter | solution.py:127
  215.7 2.2 collective-permute-start.10
  217.9 1.5 fusion.68
  219.4 0.6 fusion.64
  220.1 5.3 %fusion.19 = bf16[2,192,2048]{2,1,0:T(8,128)(2,1)} fusion(bf16[2,1024,192]{1,2,0:T(8,128)(2,1)S(1)} %copy-done.10, bf16[1024,2048]{1,0:T(8,128)(2,1)} %all-gather.5.cloned.1.call-done), kind=kOutput, calls=%fused_computation.19 | convolution fusion | flops 1611399168 | bytes 6553600 | tf_op jit(solution)/shard_map/etf,td->efd/dot_general | solution.py:135
  225.4 3.0 %fusion.16 = bf16[2,192,2048]{2,1,0:T(8,128)(2,1)} fusion(bf16[2,1024,192]{1,2,0:T(8,128)(2,1)S(1)} %copy-done.8, bf16[1024,2048]{1,0:T(8,128)(2,1)S(1)} %copy-done.17), kind=kOutput, calls=%fused_computation.18 | convolution fusion | flops 1611399168 | bytes 6553600 | tf_op jit(solution)/shard_map/etf,td->efd/dot_general | solution.py:132
  228.3 0.8 copy-done.6
  229.2 3.6 %fusion.15 = bf16[2,192,2048]{2,1,0:T(8,128)(2,1)} fusion(f32[1024,2048]{1,0:T(8,128)S(1)} %bitcast.204, f32[2,1024]{1,0:T(2,128)S(1)} %dynamic-slice_bitcast_fusion, f32[2,192,1024]{2,1,0:T(8,128)S(1)} %copy-done.6, f32[2,192,1024]{2,1,0:T(8,128)S(1)} %copy-done.4), kind=kOutput, calls=%fused_computation.17 | convolution fusion | flops 1622147072 | bytes 13115392 | tf_op jit(solution)/shard_map/etf,etd->efd/dot_general | solution.py:138
  232.7 47.3 %reduce-scatter.5.cloned.1.call-done = bf16[128,512]{1,0:T(8,128)(2,1)} async-done(((bf16[1024,512]{1,0:T(8,128)(2,1)}), bf16[128,512]{1,0:T(8,128)(2,1)}) %reduce-scatter.5.cloned.1.call-update) | async-done | bytes 131088 | tf_op jit(solution)/shard_map/reduce_scatter | solution.py:130
  280.0 9.6 %all_gather.15 = bf16[128,2048]{1,0:T(8,128)(2,1)S(1)} all-gather(bf16[128,512]{1,0:T(8,128)(2,1)} %reduce-scatter.5.cloned.1.call-done), channel_id=1, replica_groups=mesh['ctx'=8,'head'=4] {'head'}, dimensions={1}, use_global_device_ids=true | all-gather | bytes 655360 | tf_op jit(solution)/shard_map/all_gather | solution.py:131
  289.5 0.8 copy.70
  (69 shorter events, 1.0 us)
Async XLA Ops:
  7.2 76.2 %copy-start = (bf16[2,192,2048]{2,1,0:T(8,128)(2,1)S(1)}, bf16[2,192,2048]{2,1,0:T(8,128)(2,1)}, u32[]{:S(2)}) copy-start(bf16[2,192,2048]{2,1,0:T(8,128)(2,1)} %param.17) | copy-start | bytes 4718596
  7.2 76.2 %all-gather.5.cloned.1.call-start = ((), (), s32[]{:S(2)}) async-start(), calls=%async_computation.3 | async-start | bytes 4718592 | tf_op jit(solution)/shard_map/all_gather | solution.py:107
  7.9 149.2 %all-gather.3.cloned.1.call-start = ((), (), s32[]{:S(2)}) async-start(), calls=%async_computation.2 | async-start | bytes 4718592 | tf_op jit(solution)/shard_map/all_gather | solution.py:108
  8.7 207.0 %reduce-scatter.3.cloned.1.call-start = ((), (), s32[]{:S(2)}) async-start(), calls=%async_computation.4 | async-start | bytes 5242880 | tf_op jit(solution)/shard_map/reduce_scatter | solution.py:127
  32.5 56.1 %copy-start.18 = (bf16[2,192,2048]{2,1,0:T(8,128)(2,1)S(1)}, bf16[2,192,2048]{2,1,0:T(8,128)(2,1)}, u32[]{:S(2)}) copy-start(bf16[2,192,2048]{2,1,0:T(8,128)(2,1)} %param.18) | copy-start | bytes 4718596
  83.3 5.3 %copy-start.16 = (bf16[1024,2048]{1,0:T(8,128)(2,1)S(1)}, bf16[1024,2048]{1,0:T(8,128)(2,1)}, u32[]{:S(2)}) copy-start(bf16[1024,2048]{1,0:T(8,128)(2,1)} %all-gather.5.cloned.1.call-done) | copy-start | bytes 12582916
  91.6 68.9 %copy-start.2 = (bf16[2,192,2048]{2,1,0:T(8,128)(2,1)S(1)}, bf16[2,192,2048]{2,1,0:T(8,128)(2,1)}, u32[]{:S(2)}) copy-start(bf16[2,192,2048]{2,1,0:T(8,128)(2,1)} %param.19) | copy-start | bytes 4718596
  157.2 3.4 %copy-start.3 = (f32[2,192,1024]{2,1,0:T(8,128)S(1)}, f32[2,192,1024]{2,1,0:T(8,128)}, u32[]{:S(2)}) copy-start(f32[2,192,1024]{2,1,0:T(8,128)} %fusion.11) | copy-start | bytes 4718596
  157.2 3.4 %copy-start.5 = (f32[2,192,1024]{2,1,0:T(8,128)S(1)}, f32[2,192,1024]{2,1,0:T(8,128)}, u32[]{:S(2)}) copy-start(f32[2,192,1024]{2,1,0:T(8,128)} %fusion.13) | copy-start | bytes 4718596
  160.6 3.7 %copy-start.1 = (f32[1024,2048]{1,0:T(8,128)}, f32[1024,2048]{1,0:T(8,128)S(1)}, u32[]{:S(2)}) copy-start(f32[1024,2048]{1,0:T(8,128)S(1)} %convert_element_type.52) | copy-start | bytes 25165828
  164.3 2.4 copy-start.7
  164.3 2.4 copy-start.9
  164.3 2.4 copy-start.19
  171.1 0.8 copy-start.20
  171.1 3.3 %copy-start.14 = (bf16[128,128]{1,0:T(8,128)(2,1)S(1)}, bf16[128,128]{1,0:T(8,128)(2,1)}, u32[]{:S(2)}) copy-start(bf16[128,128]{1,0:T(8,128)(2,1)} %param.21) | copy-start | bytes 98308
  171.1 8.1 %copy-start.11 = (bf16[128,1024]{1,0:T(8,128)(2,1)S(1)}, bf16[128,1024]{1,0:T(8,128)(2,1)}, u32[]{:S(2)}) copy-start(bf16[128,1024]{1,0:T(8,128)(2,1)} %param.23) | copy-start | bytes 786436
  171.1 8.1 %copy-start.12 = (bf16[128,1024]{1,0:T(8,128)(2,1)S(1)}, bf16[128,1024]{1,0:T(8,128)(2,1)}, u32[]{:S(2)}) copy-start(bf16[128,1024]{1,0:T(8,128)(2,1)} %param.24) | copy-start | bytes 786436
  171.1 8.2 %copy-start.15 = (s32[1024]{0:T(1024)S(1)}, s32[1024]{0:T(1024)}, u32[]{:S(2)}) copy-start(s32[1024]{0:T(1024)} %param.25) | copy-start | bytes 12292
  171.1 12.4 %copy-start.13 = (bf16[128,1024]{1,0:T(8,128)(2,1)S(1)}, bf16[128,1024]{1,0:T(8,128)(2,1)}, u32[]{:S(2)}) copy-start(bf16[128,1024]{1,0:T(8,128)(2,1)} %param.20) | copy-start | bytes 786436
  171.1 108.9 %reduce-scatter.5.cloned.1.call-start = ((), (), s32[]{:S(2)}) async-start(), calls=%async_computation.5 | async-start | bytes 1179648 | tf_op jit(solution)/shard_map/reduce_scatter | solution.py:130
  171.8 12.5 %collective-permute-start.4 = (bf16[128,128]{1,0:T(8,128)(2,1)S(1)}, bf16[128,128]{1,0:T(8,128)(2,1)S(1)}, u32[]{:S(2)}, u32[]{:S(2)}) collective-permute-start(bf16[128,128]{1,0:T(8,128)(2,1)S(1)} %copy-done.20), channel_id=1, source_target_pairs={{0,8},{4,12},{8,16},{12,20},{16,24},{20,28},{1,9},{5,13},{9,17},{1... | collective-permute-start | bytes 98312 | tf_op jit(solution)/shard_map/ppermute | solution.py:15
  173.1 11.2 %collective-permute-start.3 = (bf16[128,128]{1,0:T(8,128)(2,1)S(1)}, bf16[128,128]{1,0:T(8,128)(2,1)S(1)}, u32[]{:S(2)}, u32[]{:S(2)}) collective-permute-start(bf16[128,128]{1,0:T(8,128)(2,1)S(1)} %copy-done.20), channel_id=1, source_target_pairs={{0,12},{4,16},{8,20},{12,24},{16,28},{1,13},{5,17},{9,21},{13,25},... | collective-permute-start | bytes 98312 | tf_op jit(solution)/shard_map/ppermute | solution.py:15
  174.4 6.2 %collective-permute-start.1 = (bf16[128,128]{1,0:T(8,128)(2,1)S(1)}, bf16[128,128]{1,0:T(8,128)(2,1)S(1)}, u32[]{:S(2)}, u32[]{:S(2)}) collective-permute-start(bf16[128,128]{1,0:T(8,128)(2,1)S(1)} %copy-done.14), channel_id=1, source_target_pairs={{0,8},{4,12},{8,16},{12,20},{16,24},{20,28},{1,9},{5,13},{9,17},{1... | collective-permute-start | bytes 98312 | tf_op jit(solution)/shard_map/ppermute | solution.py:15
  175.7 7.7 %collective-permute-start = (bf16[128,128]{1,0:T(8,128)(2,1)S(1)}, bf16[128,128]{1,0:T(8,128)(2,1)S(1)}, u32[]{:S(2)}, u32[]{:S(2)}) collective-permute-start(bf16[128,128]{1,0:T(8,128)(2,1)S(1)} %copy-done.14), channel_id=1, source_target_pairs={{0,12},{4,16},{8,20},{12,24},{16,28},{1,13},{5,17},{9,21},{13,25},... | collective-permute-start | bytes 98312 | tf_op jit(solution)/shard_map/ppermute | solution.py:15
  177.0 6.4 %collective-permute-start.2 = (bf16[128,128]{1,0:T(8,128)(2,1)S(1)}, bf16[128,128]{1,0:T(8,128)(2,1)S(1)}, u32[]{:S(2)}, u32[]{:S(2)}) collective-permute-start(bf16[128,128]{1,0:T(8,128)(2,1)S(1)} %copy-done.14), channel_id=1, source_target_pairs={{0,4},{4,8},{8,12},{12,16},{16,20},{20,24},{24,28},{1,5},{5,9},{9,... | collective-permute-start | bytes 98312 | tf_op jit(solution)/shard_map/ppermute | solution.py:15
  180.6 5.5 %collective-permute-start.5 = (bf16[128,128]{1,0:T(8,128)(2,1)S(1)}, bf16[128,128]{1,0:T(8,128)(2,1)S(1)}, u32[]{:S(2)}, u32[]{:S(2)}) collective-permute-start(bf16[128,128]{1,0:T(8,128)(2,1)S(1)} %copy-done.20), channel_id=1, source_target_pairs={{0,4},{4,8},{8,12},{12,16},{16,20},{20,24},{24,28},{1,5},{5,9},{9,... | collective-permute-start | bytes 98312 | tf_op jit(solution)/shard_map/ppermute | solution.py:15
  188.1 27.6 %collective-permute-start.6 = (f32[128,128]{1,0:T(8,128)}, f32[128,128]{1,0:T(8,128)S(1)}, u32[]{:S(2)}, u32[]{:S(2)}) collective-permute-start(f32[128,128]{1,0:T(8,128)} %get-tuple-element.26), channel_id=1, source_target_pairs={{4,0},{8,4},{12,8},{16,12},{20,16},{24,20},{28,24},{5,1},{9,5},{13... | collective-permute-start | bytes 196616 | tf_op jit(solution)/shard_map/ppermute | solution.py:15
  191.9 26.0 %collective-permute-start.8 = (f32[128,128]{1,0:T(8,128)}, f32[128,128]{1,0:T(8,128)}, u32[]{:S(2)}, u32[]{:S(2)}) collective-permute-start(f32[128,128]{1,0:T(8,128)} %get-tuple-element.27), channel_id=1, source_target_pairs={{12,0},{16,4},{20,8},{24,12},{28,16},{13,1},{17,5},{21,9},{25,13},... | collective-permute-start | bytes 196616 | tf_op jit(solution)/shard_map/ppermute | solution.py:15
  198.2 19.7 %collective-permute-start.7 = (f32[128,128]{1,0:T(8,128)S(1)}, f32[128,128]{1,0:T(8,128)}, u32[]{:S(2)}, u32[]{:S(2)}) collective-permute-start(f32[128,128]{1,0:T(8,128)S(1)} %get-tuple-element.28), channel_id=1, source_target_pairs={{8,0},{12,4},{16,8},{20,12},{24,16},{28,20},{9,1},{13,5},{17,9},{2... | collective-permute-start | bytes 196616 | tf_op jit(solution)/shard_map/ppermute | solution.py:15
  201.1 19.0 %copy-start.10 = (bf16[2,1024,192]{1,2,0:T(8,128)(2,1)S(1)}, bf16[2,1024,192]{1,2,0:T(8,128)(2,1)}, u32[]{:S(2)}) copy-start(bf16[2,1024,192]{1,2,0:T(8,128)(2,1)} %copy-done.9) | copy-start | bytes 2359300
  202.6 16.8 %collective-permute-start.9 = (f32[128,128]{1,0:T(8,128)}, f32[128,128]{1,0:T(8,128)S(1)}, u32[]{:S(2)}, u32[]{:S(2)}) collective-permute-start(f32[128,128]{1,0:T(8,128)} %get-tuple-element.23), channel_id=1, source_target_pairs={{4,0},{8,4},{12,8},{16,12},{20,16},{24,20},{28,24},{5,1},{9,5},{13... | collective-permute-start | bytes 196616 | tf_op jit(solution)/shard_map/ppermute | solution.py:15
  205.4 14.0 %collective-permute-start.11 = (f32[128,128]{1,0:T(8,128)S(1)}, f32[128,128]{1,0:T(8,128)S(1)}, u32[]{:S(2)}, u32[]{:S(2)}) collective-permute-start(f32[128,128]{1,0:T(8,128)S(1)} %get-tuple-element.24), channel_id=1, source_target_pairs={{12,0},{16,4},{20,8},{24,12},{28,16},{13,1},{17,5},{21,9},{25,13},... | collective-permute-start | bytes 196616 | tf_op jit(solution)/shard_map/ppermute | solution.py:15
  215.7 3.7 %collective-permute-start.10 = (f32[128,128]{1,0:T(8,128)S(1)}, f32[128,128]{1,0:T(8,128)S(1)}, u32[]{:S(2)}, u32[]{:S(2)}) collective-permute-start(f32[128,128]{1,0:T(8,128)S(1)} %get-tuple-element.25), channel_id=1, source_target_pairs={{8,0},{12,4},{16,8},{20,12},{24,16},{28,20},{9,1},{13,5},{17,9},{2... | collective-permute-start | bytes 196616 | tf_op jit(solution)/shard_map/ppermute | solution.py:15
  220.1 5.3 %copy-start.8 = (bf16[2,1024,192]{1,2,0:T(8,128)(2,1)S(1)}, bf16[2,1024,192]{1,2,0:T(8,128)(2,1)}, u32[]{:S(2)}) copy-start(bf16[2,1024,192]{1,2,0:T(8,128)(2,1)} %copy-done.7) | copy-start | bytes 2359300
  220.1 5.3 %copy-start.17 = (bf16[1024,2048]{1,0:T(8,128)(2,1)S(1)}, bf16[1024,2048]{1,0:T(8,128)(2,1)}, u32[]{:S(2)}) copy-start(bf16[1024,2048]{1,0:T(8,128)(2,1)} %all-gather.5.cloned.1.call-done) | copy-start | bytes 12582916
  220.1 8.3 %slice-start = ((s8[8388608]{0:T(1024)(128)(4,1)}), s8[4194304]{0:T(1024)(128)(4,1)S(1)}, s32[]{:S(2)}) async-start(s8[8388608]{0:T(1024)(128)(4,1)} %bitcast.203), calls=%async_computation.6 | async-start | bytes 8388608
  225.3 3.0 %slice-start.1 = ((s8[8388608]{0:T(1024)(128)(4,1)}), s8[4194304]{0:T(1024)(128)(4,1)S(1)}, s32[]{:S(2)}) async-start(s8[8388608]{0:T(1024)(128)(4,1)} %bitcast.203), calls=%async_computation.7 | async-start | bytes 8388608
  225.3 3.0 %copy-start.4 = (f32[2,192,1024]{2,1,0:T(8,128)S(1)}, f32[2,192,1024]{2,1,0:T(8,128)}, u32[]{:S(2)}) copy-start(f32[2,192,1024]{2,1,0:T(8,128)} %fusion.11) | copy-start | bytes 4718596
  225.4 3.8 %copy-start.6 = (f32[2,192,1024]{2,1,0:T(8,128)S(1)}, f32[2,192,1024]{2,1,0:T(8,128)}, u32[]{:S(2)}) copy-start(f32[2,192,1024]{2,1,0:T(8,128)} %fusion.13) | copy-start | bytes 4718596
Sparse Core Ops, SparseCore 0:
  10.1 73.1 all-gather.4
  85.5 71.6 all-gather.2
  171.2 44.3 reduce-scatter.2
  219.3 60.6 reduce-scatter.4

commit v2 on v1

--- a/solution.py
+++ b/solution.py
@@ -1,12 +1,15 @@
 import jax
 import jax.numpy as jnp
 from jax import lax
+from jax.experimental import pallas as pl
+from jax.experimental.pallas import tpu as pltpu
 from jax.sharding import PartitionSpec as P
 
 HQ = 32
 KVH = 4
 HD = 128
 REACH = 3
+MESH = pl.DeviceIdType.MESH
 
 
 def passed_along(block, axis, distance):
@@ -250,6 +253,416 @@
     )
 
 
+def combined_kernel(
+    tok, grd, side_in, wg, wu, wd, q_in, o_in, ga_in, vis,
+    gtok_o, gg_o, gu_o, gd_o, dq_o, dk_o, dv_o,
+    g, side, ggs, ugs, hds, send_c, recv_c, acc, send_y, recv_y, send_x, recv_x,
+    send_z, recv_z, total, fin, sgs, pls, qs, gas, kv_own, kv_send, kv_recv,
+    zs, zr, ys, yr, xs, xr, cs, cr, rcs, rcr, rys, ryr, rxs, rxr, rzs, rzr, fs, fr, ks, kr,
+):
+    f32, bf16 = jnp.float32, jnp.bfloat16
+    rows, quarter = g.shape[3], g.shape[4]
+    ctx, head = lax.axis_index("ctx"), lax.axis_index("head")
+    z, y = ctx // 2, ctx % 2
+    x, c = head // 2, head % 2
+    head_x = (1 - x) * 2 + c
+    head_c = x * 2 + (1 - c)
+    head_xc = (1 - x) * 2 + (1 - c)
+    ctx_y = z * 2 + (1 - y)
+    upper = z // 2
+    near = upper * (3 - z) + (1 - upper) * z
+    order = [upper * (3 - f) + (1 - upper) * f for f in (near, 1 - near, 2, 3)]
+    order = [jnp.int32(v) if isinstance(v, int) else v for v in order]
+
+    def remote(src, dst, send_sem, recv_sem, to_ctx, to_head):
+        return pltpu.make_async_remote_copy(
+            src_ref=src, dst_ref=dst, send_sem=send_sem, recv_sem=recv_sem,
+            device_id=(to_ctx, to_head), device_id_type=MESH,
+        )
+
+    pending = []
+
+    def send(copy, condition=None):
+        if condition is None:
+            copy.start()
+        else:
+            pl.when(condition)(copy.start)
+        pending.append((copy, condition))
+
+    barrier = pltpu.get_barrier_semaphore()
+
+    def greet(to_ctx, to_head):
+        pl.semaphore_signal(barrier, inc=1, device_id=(to_ctx, to_head), device_id_type=MESH)
+
+    for other in (head_x, head_c):
+        greet(ctx, other)
+    for away in range(1, 8):
+        greet((ctx + away) % 8, head)
+
+    def own_quarter(q):
+        cols = pl.ds(pl.multiple_of(q * quarter, quarter), quarter)
+        g[0, q, ctx] = tok[:, cols]
+        g[1, q, ctx] = grd[:, cols]
+
+    own_quarter(head)
+    side[ctx] = side_in[...]
+    pl.semaphore_wait(barrier, 9)
+
+    def piece(q, b):
+        return g.at[:, q, b]
+
+    def send_z_dir(zp, slot, to_z):
+        b = zp * 2 + y
+        there = (to_z >= 0) & (to_z < 4)
+        to_ctx = to_z * 2 + y
+        send(remote(piece(head, b), piece(head, b), zs.at[0, slot], zr.at[0, zp], to_ctx, head), there)
+        send(remote(side.at[b], side.at[b], zs.at[1, slot], zr.at[1, zp], to_ctx, head), there)
+
+    def send_y_dir(i):
+        b = order[i] * 2 + y
+        send(remote(piece(head, b), piece(head, b), ys.at[0, i], yr.at[0, i], ctx_y, head))
+        send(remote(side.at[b], side.at[b], ys.at[1, i], yr.at[1, i], ctx_y, head))
+
+    blocks = {}
+    for k, (kind, i) in enumerate(("B0", "A1", "B1", "A2", "B2", "A3", "B3")):
+        i = int(i)
+        blocks[kind + str(i)] = (k, order[i] * 2 + (y if kind == "A" else 1 - y))
+
+    def send_x_dir(name):
+        k, b = blocks[name]
+        send(remote(piece(head, b), piece(head, b), xs.at[k], xr.at[k], ctx, head_x))
+        send(remote(piece(head, b), piece(head, b), cs.at[k, 0], cr.at[k, 0], ctx, head_c))
+
+    def got_z(i):
+        zp = order[i]
+        b = zp * 2 + y
+        remote(piece(head, b), piece(head, b), zs.at[0, i], zr.at[0, zp], ctx, head).wait_recv()
+        remote(side.at[b], side.at[b], zs.at[1, i], zr.at[1, zp], ctx, head).wait_recv()
+        below = jnp.where(zp < z, 1, -1)
+        send_z_dir(zp, i + 1, z + below)
+        send_y_dir(i)
+
+    def got_y(i):
+        b = order[i] * 2 + (1 - y)
+        remote(piece(head, b), piece(head, b), ys.at[0, i], yr.at[0, i], ctx, head).wait_recv()
+        remote(side.at[b], side.at[b], ys.at[1, i], yr.at[1, i], ctx, head).wait_recv()
+
+    def got_x(name):
+        k, b = blocks[name]
+        part = piece(head_x, b)
+        remote(part, part, xs.at[k], xr.at[k], ctx, head).wait_recv()
+        send(remote(part, part, cs.at[k, 1], cr.at[k, 1], ctx, head_c))
+
+    def got_c(name):
+        k, b = blocks[name]
+        for at, q in ((0, head_c), (1, head_xc)):
+            part = piece(q, b)
+            remote(part, part, cs.at[k, at], cr.at[k, at], ctx, head).wait_recv()
+
+    def nt(a, b):
+        return lax.dot_general(a, b, (((1,), (1,)), ((), ())), preferred_element_type=f32)
+
+    def tn(a, b):
+        return lax.dot_general(a, b, (((0,), (0,)), ((), ())), preferred_element_type=f32)
+
+    units = wg.shape[0] // 2
+
+    def pair_compute(i):
+        zp = order[i]
+        pair = pl.ds(zp * 2, 2)
+        gate_pre = up_pre = hid = None
+        for q in range(4):
+            cols = slice(q * quarter, (q + 1) * quarter)
+            t = g[0, q, pair].reshape(2 * rows, quarter)
+            d = g[1, q, pair].reshape(2 * rows, quarter)
+            parts = (nt(t, wg[:, cols]), nt(t, wu[:, cols]), nt(d, wd[:, cols]))
+            if q == 0:
+                gate_pre, up_pre, hid = parts
+            else:
+                gate_pre, up_pre, hid = gate_pre + parts[0], up_pre + parts[1], hid + parts[2]
+        table = side[pair, :, 0:128].reshape(2 * rows, 128).astype(f32)
+        lane = lax.broadcasted_iota(jnp.int32, (2 * rows, 128), 1)
+        p0 = jnp.sum(jnp.where(lane == 2 * ctx, table, 0.0), axis=1, keepdims=True)
+        p1 = jnp.sum(jnp.where(lane == 2 * ctx + 1, table, 0.0), axis=1, keepdims=True)
+        unit = lax.broadcasted_iota(jnp.int32, (2 * rows, 2 * units), 1)
+        prob = jnp.where(unit < units, p0, p1)
+        hid = hid * prob
+        s = jax.nn.sigmoid(gate_pre)
+        active = gate_pre * s
+        gate_grad = (hid * up_pre * s * (1.0 + gate_pre * (1.0 - s))).astype(bf16)
+        up_grad = (hid * active).astype(bf16)
+        ggs[zp] = gate_grad
+        ugs[zp] = up_grad
+        hds[zp] = (active * up_pre * prob).astype(bf16)
+
+        def back(q):
+            cols = pl.ds(pl.multiple_of(q * quarter, quarter), quarter)
+            return jnp.dot(gate_grad, wg[:, cols], preferred_element_type=f32) + jnp.dot(
+                up_grad, wu[:, cols], preferred_element_type=f32
+            )
+
+        for xx in range(2):
+            send_c[i, xx] = back(2 * xx + (1 - c)).astype(bf16)
+        send(remote(send_c.at[i], recv_c.at[i], rcs.at[i], rcr.at[i], ctx, head_c))
+        for xx in range(2):
+            acc[i, xx] = back(2 * xx + c).reshape(2, rows, quarter)
+
+    def return_y(i):
+        remote(send_c.at[i], recv_c.at[i], rcs.at[i], rcr.at[i], ctx, head).wait_recv()
+        for xx in range(2):
+            send_y[i, xx] = (
+                acc[i, xx, 1 - y] + recv_c[i, xx, pl.ds((1 - y) * rows, rows)].astype(f32)
+            ).astype(bf16)
+        send(remote(send_y.at[i], recv_y.at[i], rys.at[i], ryr.at[i], ctx_y, head))
+
+    def return_x(i):
+        remote(send_y.at[i], recv_y.at[i], rys.at[i], ryr.at[i], ctx, head).wait_recv()
+
+        def mine(xx):
+            return (
+                acc[i, xx, y]
+                + recv_c[i, xx, pl.ds(y * rows, rows)].astype(f32)
+                + recv_y[i, xx].astype(f32)
+            )
+
+        send_x[i] = mine(1 - x).astype(bf16)
+        send(remote(send_x.at[i], recv_x.at[i], rxs.at[i], rxr.at[i], ctx, head_x))
+        total[i] = mine(x)
+
+    def return_z(i):
+        remote(send_x.at[i], recv_x.at[i], rxs.at[i], rxr.at[i], ctx, head).wait_recv()
+        value = total[i] + recv_x[i].astype(f32)
+        if i == 0:
+            total[i] = value
+        else:
+            send_z[i] = value.astype(bf16)
+            send(remote(
+                send_z.at[i], recv_z.at[z], rzs.at[i], rzr.at[z], order[i] * 2 + y, head
+            ))
+
+    scale = HD ** (-0.5)
+    heads = q_in.shape[1] // HD
+
+    def attention():
+        starts = [jnp.maximum(ctx - j, 0) for j in (3, 2, 1, 0)]
+        key = jnp.concatenate([side[b, :, 128:256] for b in starts], axis=0)
+        value = jnp.concatenate([side[b, :, 256:384] for b in starts], axis=0)
+        seen = vis[...] > 0
+        for h in range(heads):
+            cols = slice(h * HD, (h + 1) * HD)
+            at = slice(h * rows, (h + 1) * rows)
+            qh, gh = q_in[:, cols], ga_in[:, cols]
+            qs[at, :] = qh
+            gas[at, :] = gh
+            scores = jnp.where(seen, nt(qh, key) * scale, -jnp.inf)
+            peak = jnp.max(scores, axis=1, keepdims=True)
+            weight = jnp.exp(scores - peak)
+            probs = weight / jnp.sum(weight, axis=1, keepdims=True)
+            delta = jnp.sum(
+                gh.astype(f32) * o_in[:, cols].astype(f32), axis=1, keepdims=True
+            )
+            sg = (probs * (nt(gh, value) - delta)).astype(bf16)
+            sgs[at, :] = sg
+            pls[at, :] = probs.astype(bf16)
+            dq_o[:, cols] = (
+                scale * jnp.dot(sg, key, preferred_element_type=f32)
+            ).astype(bf16)
+        key_terms = scale * tn(sgs[...], qs[...])
+        value_terms = tn(pls[...], gas[...])
+        for j in (1, 2, 3):
+            at = slice((3 - j) * rows, (4 - j) * rows)
+            kv_send[j - 1, :, 0:HD] = key_terms[at]
+            kv_send[j - 1, :, HD : 2 * HD] = value_terms[at]
+            send(
+                remote(kv_send.at[j - 1], kv_recv.at[j - 1], ks.at[j - 1], kr.at[j - 1], ctx - j, head),
+                ctx - j >= 0,
+            )
+        kv_own[:, 0:HD] = key_terms[3 * rows :]
+        kv_own[:, HD : 2 * HD] = value_terms[3 * rows :]
+
+    def attention_end():
+        for j in (1, 2, 3):
+
+            @pl.when(ctx + j < 8)
+            def _():
+                remote(
+                    kv_send.at[j - 1], kv_recv.at[j - 1], ks.at[j - 1], kr.at[j - 1], ctx, head
+                ).wait_recv()
+                kv_own[...] += kv_recv[j - 1]
+
+        dk_o[...] = kv_own[:, 0:HD].astype(bf16)
+        dv_o[...] = kv_own[:, HD : 2 * HD].astype(bf16)
+
+    def weight_grad(source, which, out):
+        flat = source[...].reshape(8 * rows, 2 * units)
+        for q in range(4):
+            cols = slice(q * quarter, (q + 1) * quarter)
+            out[:, cols] = tn(flat, g[which, q].reshape(8 * rows, quarter)).astype(bf16)
+
+    send_z_dir(z, 0, z + 1)
+    send_z_dir(z, 1, z - 1)
+    send_y_dir(0)
+    for away in (1, 2, 3):
+        own_quarter((head + away) % 4)
+    got_y(0)
+    send_x_dir("B0")
+    got_z(1)
+    send_x_dir("A1")
+    got_z(2)
+    got_y(1)
+    send_x_dir("B1")
+    send_x_dir("A2")
+    got_x("B0")
+    got_c("B0")
+    pair_compute(0)
+    got_z(3)
+    got_y(2)
+    send_x_dir("B2")
+    send_x_dir("A3")
+    got_y(3)
+    send_x_dir("B3")
+    got_x("A1")
+    return_y(0)
+    attention()
+    for name in ("B1", "A2"):
+        got_x(name)
+    got_c("A1")
+    got_c("B1")
+    pair_compute(1)
+    return_x(0)
+    got_x("B2")
+    got_c("A2")
+    got_c("B2")
+    return_y(1)
+    pair_compute(2)
+    return_z(0)
+    return_x(1)
+    got_x("A3")
+    got_x("B3")
+    got_c("A3")
+    got_c("B3")
+    return_y(2)
+    pair_compute(3)
+    return_z(1)
+    return_x(2)
+    weight_grad(ggs, 0, gg_o)
+    return_y(3)
+    return_z(2)
+    attention_end()
+    return_x(3)
+    weight_grad(ugs, 0, gu_o)
+    return_z(3)
+    weight_grad(hds, 1, gd_o)
+    result = total[0]
+    for j in (1, 2, 3):
+        other = (z + j) % 4
+        remote(send_z.at[j], recv_z.at[other], rzs.at[j], rzr.at[other], ctx, head).wait_recv()
+        result = result + recv_z[other].astype(f32)
+    fin[head] = result.astype(bf16)
+    send(remote(fin.at[head], fin.at[head], fs.at[0], fr.at[0], ctx, head_x))
+    send(remote(fin.at[head], fin.at[head], fs.at[1], fr.at[1], ctx, head_c))
+    remote(fin.at[head_x], fin.at[head_x], fs.at[0], fr.at[0], ctx, head).wait_recv()
+    send(remote(fin.at[head_x], fin.at[head_x], fs.at[2], fr.at[2], ctx, head_c))
+    remote(fin.at[head_c], fin.at[head_c], fs.at[1], fr.at[1], ctx, head).wait_recv()
+    remote(fin.at[head_xc], fin.at[head_xc], fs.at[2], fr.at[2], ctx, head).wait_recv()
+    for q in range(4):
+        gtok_o[:, q * quarter : (q + 1) * quarter] = fin[q]
+    for copy, condition in pending:
+        if condition is None:
+            copy.wait_send()
+        else:
+            pl.when(condition)(copy.wait_send)
+
+
+def combined_body(
+    tokens, grad_out, expert_ids, gate_probs, w_gate, w_up, w_down,
+    query_rows, key_rows, value_rows, attn_out, grad_attn, segment_ids,
+):
+    rows, width = tokens.shape
+    local_experts, units, _ = w_gate.shape
+    quarter = width // 4
+    f32, bf16 = jnp.float32, jnp.bfloat16
+    chosen = expert_ids[:, :, None] == jnp.arange(128, dtype=jnp.int32)[None, None, :]
+    table = jnp.sum(jnp.where(chosen, gate_probs.astype(f32)[:, :, None], 0.0), axis=1).astype(bf16)
+    side_rows = jnp.concatenate([table, key_rows, value_rows], axis=1)
+    window = (REACH + 1) * rows
+    ctx_index = lax.axis_index("ctx")
+    query_pos = ctx_index * rows + jnp.arange(rows, dtype=jnp.int32)
+    key_pos = (ctx_index - REACH) * rows + jnp.arange(window, dtype=jnp.int32)
+    padded_segment = jnp.concatenate([jnp.full((REACH * rows,), -1, jnp.int32), segment_ids])
+    key_seg = lax.dynamic_slice_in_dim(padded_segment, ctx_index * rows, window, 0)
+    query_seg = lax.dynamic_slice_in_dim(segment_ids, ctx_index * rows, rows, 0)
+    visible = (
+        (key_pos[None, :] <= query_pos[:, None]) & (key_seg[None, :] == query_seg[:, None])
+    ).astype(f32)
+    both = local_experts * units
+    flat = [w.reshape(both, width) for w in (w_gate, w_up, w_down)]
+    vmem = pl.BlockSpec(memory_space=pltpu.VMEM)
+    dma = pltpu.SemaphoreType.DMA
+    att_width = query_rows.shape[1]
+    shapes = [
+        (rows, width), (both, width), (both, width), (both, width),
+        (rows, att_width), (rows, HD), (rows, HD),
+    ]
+    stacked = rows * (att_width // HD)
+    outs = pl.pallas_call(
+        combined_kernel,
+        out_shape=[jax.ShapeDtypeStruct(s, bf16) for s in shapes],
+        in_specs=[vmem] * 10,
+        out_specs=[vmem] * 7,
+        scratch_shapes=[
+            pltpu.VMEM((2, 4, 8, rows, quarter), bf16),
+            pltpu.VMEM((8, rows, 384), bf16),
+            pltpu.VMEM((4, 2 * rows, both), bf16),
+            pltpu.VMEM((4, 2 * rows, both), bf16),
+            pltpu.VMEM((4, 2 * rows, both), bf16),
+            pltpu.VMEM((4, 2, 2 * rows, quarter), bf16),
+            pltpu.VMEM((4, 2, 2 * rows, quarter), bf16),
+            pltpu.VMEM((4, 2, 2, rows, quarter), f32),
+            pltpu.VMEM((4, 2, rows, quarter), bf16),
+            pltpu.VMEM((4, 2, rows, quarter), bf16),
+            pltpu.VMEM((4, rows, quarter), bf16),
+            pltpu.VMEM((4, rows, quarter), bf16),
+            pltpu.VMEM((4, rows, quarter), bf16),
+            pltpu.VMEM((4, rows, quarter), bf16),
+            pltpu.VMEM((4, rows, quarter), f32),
+            pltpu.VMEM((4, rows, quarter), bf16),
+            pltpu.VMEM((stacked, window), bf16),
+            pltpu.VMEM((stacked, window), bf16),
+            pltpu.VMEM((stacked, HD), bf16),
+            pltpu.VMEM((stacked, HD), bf16),
+            pltpu.VMEM((rows, 2 * HD), f32),
+            pltpu.VMEM((3, rows, 2 * HD), f32),
+            pltpu.VMEM((3, rows, 2 * HD), f32),
+            dma((2, 5)), dma((2, 4)), dma((2, 4)), dma((2, 4)),
+            dma((7,)), dma((7,)), dma((7, 2)), dma((7, 2)),
+            dma((4,)), dma((4,)), dma((4,)), dma((4,)), dma((4,)), dma((4,)),
+            dma((4,)), dma((4,)), dma((3,)), dma((3,)), dma((3,)), dma((3,)),
+        ],
+        compiler_params=pltpu.CompilerParams(
+            collective_id=0, has_side_effects=True, vmem_limit_bytes=58 * 1024 * 1024
+        ),
+        cost_estimate=pl.CostEstimate(
+            flops=8 * 2 * 8 * rows * width * both, bytes_accessed=6 * both * width * 2,
+            transcendentals=0,
+        ),
+    )(tokens, grad_out, side_rows, *flat, query_rows, attn_out, grad_attn, visible)
+    grads = [w.reshape(local_experts, units, width) for w in outs[1:4]]
+    return (outs[0], *grads, *outs[4:])
+
+
+def chosen_body(*blocks):
+    tokens, expert_ids, w_gate, query_rows = blocks[0], blocks[2], blocks[4], blocks[7]
+    ctx_count, head_count = lax.axis_size("ctx"), lax.axis_size("head")
+    pairs = 5 * tokens.shape[0] * expert_ids.shape[1]
+    slots = w_gate.shape[0] * -(-pairs // (4 * w_gate.shape[0] * ctx_count))
+    fits = ctx_count == 8 and head_count == 4 and w_gate.shape[0] == 2
+    same_rows = tokens.shape[0] == query_rows.shape[0] and blocks[8].shape[1] == HD
+    if fits and same_rows and slots >= tokens.shape[0]:
+        return combined_body(*blocks)
+    return body(*blocks)
+
+
 def solution(mesh):
     placed = (
         P("ctx", None),
@@ -267,7 +680,7 @@
         P(),
     )
     return jax.shard_map(
-        body,
+        chosen_body,
         mesh=mesh,
         in_specs=placed,
         out_specs=(

time: 300 us -> 122 us (0.41)
  waiting for transfers between devices: 177 us -> 0 us
  Pallas kernels: 0 us -> 105 us
  matrix products: 33.1 us -> 0 us
  blocking collectives: 31.9 us -> 0 us
  starting transfers between devices: 27.8 us -> 0 us
  between operations: 14.2 us -> 0.66 us
  local copies, waits for them, and re-layouts: 4.72 us -> 12.1 us
  other arithmetic: 7.86 us -> 3.36 us
    all_gather x2 -> x0, waiting for transfers between devices: 116 us -> none  [the longest x1 65.5 us: dense_experts(): all_grads = lax.all_gather(grad_out, 'ctx', axis=0, tiled=True)]
    pallas_call x0 -> x1, Pallas kernels: none -> 105 us  [combined_body(): pl.pallas_call(combined_kernel, out_shape=[jax.ShapeDtypeStruct(s, bf16)...]
    reduce_scatter x2 -> x0, waiting for transfers between devices: 56.2 us -> none  [the longest x1 47.3 us: dense_experts(): summed = lax.psum_scatter(shared, 'ctx', scatter_dimension=0, tiled=True)]
    dot_general x13 -> x0, matrix products: 33.1 us -> none  [the longest x1 5.3 us: dense_experts(): jnp.einsum('td,efd->etf', all_tokens, w_gate, preferred_element_type=jnp....]
    all_gather x2 -> x0, blocking collectives: 31.9 us -> none  [the longest x1 22.4 us: dense_experts(): all_probs = lax.all_gather(prob_table, 'ctx', axis=0, tiled=True)]
    ppermute x12 -> x0, starting transfers between devices: 27.7 us -> none  [passed_along(): return lax.ppermute(block, axis, route)]
    unnamed x50 -> x18, local copies, waits for them, and re-layouts: 3.29 us -> 10.6 us
    convert_element_type x4 -> x1, other arithmetic: 6.22 us -> 0.81 us  [combined_body(): visible = ((key_pos[None, :] <= query_pos[:, None]) & (key_seg[None, :] =...]
  transfers between devices with their start and end apart: 16 -> 0, of which waited for: 7 -> 0; matrix products, arithmetic and copies ran while one was open for 10% -> 0% of each run, Pallas kernels for 0% -> 0%
where the time goes in v2:
time: 122 us; the launch traced here: 121 us
  Pallas kernels  105 us (86%)
  local copies, waits for them, and re-layouts  12.1 us (10%)
  other arithmetic  3.36 us (3%)
    pallas_call x1, Pallas kernels, combined_body(): pl.pallas_call(combined_kernel, out_shape=[jax.ShapeDtypeStruct(s, bf16)...  105 us
    unnamed x18, local copies, waits for them, and re-layouts  10.6 us

profile of v2, /device:TPU:25, one launch (start us, length us, event | category | flops | bytes accessed | tf_op | source)
XLA Modules:
  0.0 121.4 jit_solution(10381054783983110833)
XLA Ops:
  0.6 0.8 dynamic_slice.7
  1.4 0.8 pad_dynamic-slice_fusion
  2.2 0.8 copy.22
  3.0 0.8 copy.23
  3.7 0.4 select_reduce_fusion
  4.1 1.4 %pad_maximum_fusion.side_in = bf16[128,384]{1,0:T(8,128)(2,1)} fusion(bf16[128,128]{1,0:T(8,128)(2,1)} %param.22, bf16[128,128]{1,0:T(8,128)(2,1)} %param.21, bf16[128,128]{1,0:T(8,128)(2,1)S(1)} %select_reduce_fusion), kind=kLoop, calls=%fused_computation.3 | loop fusion | flops 294912 | bytes 196608 | tf_op jit(solution)/shard_map/concatenate | solution.py:587
  5.5 0.8 and_convert_fusion.vis
  6.3 105.2 %shard_map.180 = (bf16[128,2048]{1,0:T(8,128)(2,1)}, bf16[384,2048]{1,0:T(8,128)(2,1)}, bf16[384,2048]{1,0:T(8,128)(2,1)}, bf16[384,2048]{1,0:T(8,128)(2,1)}, bf...) custom-call(bf16[128,2048]{1,0:T(8,128)(2,1)} %tok.1, bf16[128,2048]{1,0:T(8,128)(2,1)} %grd.1, ...), custom_call_target="tpu_custom_call" | custom-call | flops 12884901888 | bytes 9437184 | tf_op jit(solution)/shard_map/pallas_call | solution.py:608
  111.6 1.9 %copy.31 = bf16[128,2048]{1,0:T(8,128)(2,1)} copy(bf16[128,2048]{1,0:T(8,128)(2,1)} %get-tuple-element.30) | data formatting | bytes 1048576
  113.5 0.0 copy-start.1
  113.5 2.8 %copy.32 = bf16[2,192,2048]{2,1,0:T(8,128)(2,1)} copy(bf16[2,192,2048]{2,1,0:T(8,128)(2,1)} %bitcast.8) | data formatting | bytes 3145728
  116.3 0.0 copy-done.1
  116.3 0.0 copy-start
  116.3 1.1 copy.33
  117.5 0.8 copy-done
  118.3 0.0 copy-start.2
  118.3 0.0 copy-start.4
  118.3 0.0 copy-start.3
  118.3 1.1 copy.34
  119.5 0.0 copy-done.2
  119.5 0.7 copy.35
  120.2 0.0 copy-done.4
  120.2 0.6 copy.36
  120.8 0.0 copy-done.3
  120.8 0.6 copy.37
  (1 shorter events, 0.0 us)
Async XLA Ops:
  113.5 2.9 %copy-start.1 = (bf16[384,2048]{1,0:T(8,128)(2,1)S(1)}, bf16[384,2048]{1,0:T(8,128)(2,1)}, u32[]{:S(2)}) copy-start(bf16[384,2048]{1,0:T(8,128)(2,1)} %get-tuple-element.16) | copy-start | bytes 4718596
  116.3 2.0 %copy-start = (bf16[384,2048]{1,0:T(8,128)(2,1)S(1)}, bf16[384,2048]{1,0:T(8,128)(2,1)}, u32[]{:S(2)}) copy-start(bf16[384,2048]{1,0:T(8,128)(2,1)} %get-tuple-element.17) | copy-start | bytes 4718596
  118.3 1.2 copy-start.2
  118.3 1.9 %copy-start.4 = (bf16[128,128]{1,0:T(8,128)(2,1)S(1)}, bf16[128,128]{1,0:T(8,128)(2,1)}, u32[]{:S(2)}) copy-start(bf16[128,128]{1,0:T(8,128)(2,1)} %get-tuple-element.35) | copy-start | bytes 98308
  118.3 2.5 %copy-start.3 = (bf16[128,128]{1,0:T(8,128)(2,1)S(1)}, bf16[128,128]{1,0:T(8,128)(2,1)}, u32[]{:S(2)}) copy-start(bf16[128,128]{1,0:T(8,128)(2,1)} %get-tuple-element.36) | copy-start | bytes 98308

commit v3 on v2

--- a/solution.py
+++ b/solution.py
@@ -257,7 +257,7 @@
     tok, grd, side_in, wg, wu, wd, q_in, o_in, ga_in, vis,
     gtok_o, gg_o, gu_o, gd_o, dq_o, dk_o, dv_o,
     g, side, ggs, ugs, hds, send_c, recv_c, acc, send_y, recv_y, send_x, recv_x,
-    send_z, recv_z, total, fin, sgs, pls, qs, gas, kv_own, kv_send, kv_recv,
+    send_z, recv_z, total, fin, sgs, pls, qs, gas, kv_own, kv_send, kv_recv, wacc,
     zs, zr, ys, yr, xs, xr, cs, cr, rcs, rcr, rys, ryr, rxs, rxr, rzs, rzr, fs, fr, ks, kr,
 ):
     f32, bf16 = jnp.float32, jnp.bfloat16
@@ -493,11 +493,20 @@
         dk_o[...] = kv_own[:, 0:HD].astype(bf16)
         dv_o[...] = kv_own[:, HD : 2 * HD].astype(bf16)
 
-    def weight_grad(source, which, out):
-        flat = source[...].reshape(8 * rows, 2 * units)
+    def half_terms(source, which, q, half):
+        flat = source[pl.ds(2 * half, 2)].reshape(4 * rows, 2 * units)
+        return tn(flat, g[which, q, pl.ds(4 * half, 4)].reshape(4 * rows, quarter))
+
+    def first_half(source, which, at):
+        for q in range(4):
+            wacc[at, :, q * quarter : (q + 1) * quarter] = half_terms(source, which, q, upper)
+
+    def weight_grad(source, which, at, out):
         for q in range(4):
             cols = slice(q * quarter, (q + 1) * quarter)
-            out[:, cols] = tn(flat, g[which, q].reshape(8 * rows, quarter)).astype(bf16)
+            out[:, cols] = (
+                wacc[at, :, cols] + half_terms(source, which, q, 1 - upper)
+            ).astype(bf16)
 
     send_z_dir(z, 0, z + 1)
     send_z_dir(z, 1, z - 1)
@@ -530,6 +539,7 @@
     got_c("B1")
     pair_compute(1)
     return_x(0)
+    first_half(ggs, 0, 0)
     got_x("B2")
     got_c("A2")
     got_c("B2")
@@ -537,7 +547,9 @@
     pair_compute(2)
     return_z(0)
     return_x(1)
+    first_half(ugs, 0, 1)
     got_x("A3")
+    first_half(hds, 1, 2)
     got_x("B3")
     got_c("A3")
     got_c("B3")
@@ -545,14 +557,14 @@
     pair_compute(3)
     return_z(1)
     return_x(2)
-    weight_grad(ggs, 0, gg_o)
+    weight_grad(ggs, 0, 0, gg_o)
     return_y(3)
     return_z(2)
     attention_end()
     return_x(3)
-    weight_grad(ugs, 0, gu_o)
+    weight_grad(ugs, 0, 1, gu_o)
     return_z(3)
-    weight_grad(hds, 1, gd_o)
+    weight_grad(hds, 1, 2, gd_o)
     result = total[0]
     for j in (1, 2, 3):
         other = (z + j) % 4
@@ -634,6 +646,7 @@
             pltpu.VMEM((rows, 2 * HD), f32),
             pltpu.VMEM((3, rows, 2 * HD), f32),
             pltpu.VMEM((3, rows, 2 * HD), f32),
+            pltpu.VMEM((3, both, width), f32),
             dma((2, 5)), dma((2, 4)), dma((2, 4)), dma((2, 4)),
             dma((7,)), dma((7,)), dma((7, 2)), dma((7, 2)),
             dma((4,)), dma((4,)), dma((4,)), dma((4,)), dma((4,)), dma((4,)),

time: 122 us -> 124 us (1.016)
  Pallas kernels: 105 us -> 107 us
    pallas_call x1, Pallas kernels: 105 us -> 107 us  [combined_body(): pl.pallas_call(combined_kernel, out_shape=[jax.ShapeDtypeStruct(s, bf16)...]
where the time goes in v3:
time: 124 us
  Pallas kernels  107 us (86%)
  local copies, waits for them, and re-layouts  12.1 us (10%)
  other arithmetic  3.36 us (3%)
    pallas_call x1, Pallas kernels, combined_body(): pl.pallas_call(combined_kernel, out_shape=[jax.ShapeDtypeStruct(s, bf16)...  107 us
    unnamed x18, local copies, waits for them, and re-layouts  10.6 us

profile of v3, /device:TPU:25, one launch (start us, length us, event | category | flops | bytes accessed | tf_op | source)
XLA Modules:
  0.0 123.5 jit_solution(7169600843015965286)
XLA Ops:
  0.6 0.8 dynamic_slice.7
  1.4 0.8 pad_dynamic-slice_fusion
  2.2 0.8 copy.22
  3.0 0.8 copy.23
  3.7 0.4 select_reduce_fusion
  4.1 1.4 %pad_maximum_fusion.side_in = bf16[128,384]{1,0:T(8,128)(2,1)} fusion(bf16[128,128]{1,0:T(8,128)(2,1)} %param.22, bf16[128,128]{1,0:T(8,128)(2,1)} %param.21, bf16[128,128]{1,0:T(8,128)(2,1)S(1)} %select_reduce_fusion), kind=kLoop, calls=%fused_computation.3 | loop fusion | flops 294912 | bytes 196608 | tf_op jit(solution)/shard_map/concatenate | solution.py:599
  5.5 0.8 and_convert_fusion.vis
  6.3 107.4 %shard_map.180 = (bf16[128,2048]{1,0:T(8,128)(2,1)}, bf16[384,2048]{1,0:T(8,128)(2,1)}, bf16[384,2048]{1,0:T(8,128)(2,1)}, bf16[384,2048]{1,0:T(8,128)(2,1)}, bf...) custom-call(bf16[128,2048]{1,0:T(8,128)(2,1)} %tok.1, bf16[128,2048]{1,0:T(8,128)(2,1)} %grd.1, ...), custom_call_target="tpu_custom_call" | custom-call | flops 12884901888 | bytes 9437184 | tf_op jit(solution)/shard_map/pallas_call | solution.py:620
  113.7 1.9 %copy.31 = bf16[128,2048]{1,0:T(8,128)(2,1)} copy(bf16[128,2048]{1,0:T(8,128)(2,1)} %get-tuple-element.30) | data formatting | bytes 1048576
  115.6 0.0 copy-start.1
  115.6 2.8 %copy.32 = bf16[2,192,2048]{2,1,0:T(8,128)(2,1)} copy(bf16[2,192,2048]{2,1,0:T(8,128)(2,1)} %bitcast.8) | data formatting | bytes 3145728
  118.4 0.0 copy-done.1
  118.4 0.0 copy-start
  118.5 1.1 copy.33
  119.6 0.8 copy-done
  120.4 0.0 copy-start.2
  120.4 0.0 copy-start.4
  120.4 0.0 copy-start.3
  120.4 1.1 copy.34
  121.6 0.0 copy-done.2
  121.6 0.7 copy.35
  122.3 0.0 copy-done.4
  122.3 0.6 copy.36
  122.9 0.0 copy-done.3
  122.9 0.6 copy.37
  (1 shorter events, 0.0 us)
Async XLA Ops:
  115.6 2.9 %copy-start.1 = (bf16[384,2048]{1,0:T(8,128)(2,1)S(1)}, bf16[384,2048]{1,0:T(8,128)(2,1)}, u32[]{:S(2)}) copy-start(bf16[384,2048]{1,0:T(8,128)(2,1)} %get-tuple-element.16) | copy-start | bytes 4718596
  118.4 2.0 %copy-start = (bf16[384,2048]{1,0:T(8,128)(2,1)S(1)}, bf16[384,2048]{1,0:T(8,128)(2,1)}, u32[]{:S(2)}) copy-start(bf16[384,2048]{1,0:T(8,128)(2,1)} %get-tuple-element.17) | copy-start | bytes 4718596
  120.4 1.2 copy-start.2
  120.4 1.9 %copy-start.4 = (bf16[128,128]{1,0:T(8,128)(2,1)S(1)}, bf16[128,128]{1,0:T(8,128)(2,1)}, u32[]{:S(2)}) copy-start(bf16[128,128]{1,0:T(8,128)(2,1)} %get-tuple-element.35) | copy-start | bytes 98308
  120.4 2.5 %copy-start.3 = (bf16[128,128]{1,0:T(8,128)(2,1)S(1)}, bf16[128,128]{1,0:T(8,128)(2,1)}, u32[]{:S(2)}) copy-start(bf16[128,128]{1,0:T(8,128)(2,1)} %get-tuple-element.36) | copy-start | bytes 98308
